TPU v7x, 256 devices: a whole 4x4x8 slice. The times are simulated.
256 devices in a mesh: freq: 64 (over z, y, core), bl: 4 (over x).
Axes of the slice: x: 4, y: 4, z: 8, core: 2. Of those that a mesh axis runs over, the one named last changes fastest.
Arguments:
- visibilities: float32 [2, 128, 2, 2048], P(None, 'freq', None, 'bl'), may hold values from -6 to 6
- coherencies: bfloat16 [2, 128, 2, 100, 2048], P(None, 'freq', None, None, 'bl'), may hold values from -0.59765625 to 0.59765625
- station_pairs: int32 [2, 2048], P(None, 'bl'), may hold values from 0 to 61, as said below
- row_flags: int32 [128, 2048], P('freq', 'bl'), may hold values 0 or 1
- gains_in: float32 [2, 128, 2, 100, 62], P(None, 'freq'), may hold values from -4 to 4
- consensus_in: float32 [2, 128, 2, 100, 62], P(None, 'freq'), may hold values from -4 to 4
- dual_in: float32 [2, 128, 2, 100, 62], P(None, 'freq'), may hold values from -2 to 2
- penalty: float32 [100], replicated, may hold values from 1 to 10
- damping: float32 [4], replicated, may hold values from 0.5 to 4
Outputs:
- gains_out: float32 [2, 128, 2, 100, 62], P(None, 'freq')
- consensus_out: float32 [2, 128, 2, 100, 62], P(None, 'freq')
- dual_out: float32 [2, 128, 2, 100, 62], P(None, 'freq')
Inputs may be any that keep to these rules, and one draw needn't show every extreme that they name: `station_pairs`: each sample names two different stations.
All inputs are finite; a program needn't handle non-finite values. No bound on the sum of `row_flags` on one device may be relied on, other than what follows from the above.
Results may differ from a plain program's by a relative error of at most 0.0003.
Values sent between devices are 32-bit elements; how exact they have to be, the bound alone decides.
A program may use at most 64 MiB of HBM per device.

v0:
```python
import jax
import jax.numpy as jnp
from jax import lax
from jax.sharding import PartitionSpec as P

HIGH = lax.Precision.HIGHEST


def bernstein(position):
    other = 1.0 - position
    return jnp.stack(
        [
            other * other * other,
            3.0 * position * other * other,
            3.0 * position * position * other,
            position * position * position,
        ],
        axis=-1,
    )


def gather_rows(values, one_hot):
    return jnp.einsum("...s,sr->...r", values, one_hot, precision=HIGH)


def to_stations(values, one_hot):
    return jnp.einsum("...r,sr->...s", values, one_hot, precision=HIGH)


def normal_terms(visibilities, coherencies, weight, gains, first_hot, second_hot):
    first = gather_rows(gains, first_hot)
    second = gather_rows(gains, second_hot)
    coh_re = coherencies[0].astype(jnp.float32)
    coh_im = coherencies[1].astype(jnp.float32)
    tre = coh_re * second[0] + coh_im * second[1]
    tim = coh_im * second[0] - coh_re * second[1]
    model_re = jnp.sum(first[0] * tre - first[1] * tim, axis=-2)
    model_im = jnp.sum(first[0] * tim + first[1] * tre, axis=-2)
    res_re = ((visibilities[0] - model_re) * weight)[..., None, :]
    res_im = ((visibilities[1] - model_im) * weight)[..., None, :]
    sre = coh_re * first[0] - coh_im * first[1]
    sim = coh_re * first[1] + coh_im * first[0]
    num_first = jnp.stack([res_re * tre + res_im * tim, res_im * tre - res_re * tim])
    num_second = jnp.stack([res_re * sre + res_im * sim, res_re * sim - res_im * sre])
    wide = weight[..., None, :]
    numer = to_stations(num_first, first_hot) + to_stations(num_second, second_hot)
    curv = to_stations(wide * (tre * tre + tim * tim), first_hot) + to_stations(
        wide * (sre * sre + sim * sim), second_hot
    )
    return (numer, curv)


def lm_update(gains, target, numer, curv, rate, damp):
    return gains + (numer - rate * (gains - target)) / (curv + damp + rate)


def fit_coeffs(basis_all, total):
    gram = jnp.dot(basis_all.T, basis_all, precision=HIGH)
    factor = jnp.linalg.cholesky(gram)
    flat = total.reshape(4, -1)
    forward = []
    for row in range(4):
        acc = flat[row]
        for col in range(row):
            acc = acc - factor[row, col] * forward[col]
        forward.append(acc / factor[row, row])
    backward = [None, None, None, None]
    for row in range(3, -1, -1):
        acc = forward[row]
        for col in range(row + 1, 4):
            acc = acc - factor[col, row] * backward[col]
        backward[row] = acc / factor[row, row]
    return jnp.stack(backward).reshape(total.shape)


def shards(
    visibilities,
    coherencies,
    station_pairs,
    row_flags,
    gains_in,
    consensus_in,
    dual_in,
    penalty,
    damping,
):
    stations = gains_in.shape[-1]
    chans = gains_in.shape[1]
    station_ids = lax.broadcasted_iota(jnp.int32, (stations, station_pairs.shape[1]), 0)
    first_hot = (station_ids == station_pairs[0][None, :]).astype(jnp.float32)
    second_hot = (station_ids == station_pairs[1][None, :]).astype(jnp.float32)
    weight = row_flags.astype(jnp.float32)[:, None, :]
    target = consensus_in - dual_in
    rate = penalty[:, None]
    gains = gains_in
    for step in range(damping.shape[0]):
        numer, curv = normal_terms(visibilities, coherencies, weight, gains, first_hot, second_hot)
        numer, curv = lax.psum((numer, curv), "bl")
        gains = lm_update(gains, target, numer, curv, rate, damping[step])
    total_chans = chans * lax.axis_size("freq")
    every = (lax.iota(jnp.int32, total_chans).astype(jnp.float32) + 0.5) / total_chans
    local = (
        (lax.axis_index("freq") * chans + lax.iota(jnp.int32, chans)).astype(jnp.float32) + 0.5
    ) / total_chans
    basis_all = bernstein(every)
    basis = bernstein(local)
    blend = gains + dual_in
    partial_value = jnp.einsum("fm,cfpks->mcpks", basis, blend, precision=HIGH)
    total = lax.psum(partial_value, "freq")
    coeffs = fit_coeffs(basis_all, total)
    consensus = jnp.einsum("fm,mcpks->cfpks", basis, coeffs, precision=HIGH)
    dual = dual_in + gains - consensus
    return (gains, consensus, dual)


def solution(mesh):
    placed = (
        P(None, "freq", None, "bl"),
        P(None, "freq", None, None, "bl"),
        P(None, "bl"),
        P("freq", "bl"),
        P(None, "freq", None, None, None),
        P(None, "freq", None, None, None),
        P(None, "freq", None, None, None),
        P(),
        P(),
    )
    return jax.shard_map(
        shards,
        mesh=mesh,
        in_specs=placed,
        out_specs=(
            P(None, "freq", None, None, None),
            P(None, "freq", None, None, None),
            P(None, "freq", None, None, None),
        ),
        check_vma=False,
    )
```

profile of v0, /device:TPU:1, one launch (start us, length us, event | category | flops | bytes accessed | tf_op | source)
XLA Modules:
  0.0 453.9 jit_solution(5521647710696413006)
XLA Ops:
  7.2 0.8 convert_element_type.113
  8.0 0.8 fusion.322
  8.7 1.7 fusion.321
  10.4 0.9 convolution_bitcast_fusion.1
  11.3 0.9 convolution_bitcast_fusion
  12.2 0.6 fusion.160
  12.8 0.7 fusion.179
  13.5 1.6 convolution_add_fusion.3
  15.1 0.7 multiply_add_fusion.6
  15.9 1.1 fusion.32
  17.0 1.8 fusion.73
  19.1 0.6 fusion.324
  19.7 48.4 %all-reduce.18.cloned.1.call-done = (f32[2,2,2,100,62]{3,4,2,1,0:T(8,128)}, f32[2,2,100,62]{2,3,1,0:T(8,128)}) async-done(((f32[2,2,2,100,62]{3,4,2,1,0:T(8,128)}, f32[2,2,100,62]{2,3,1,0:T(8,128)}), (f32[2,2,2,100,62]{3,4,2,1,0:T(8,128)}, f32[2,2,100,62]{2,3,1,0:T(8,128)})) %all-reduce.18.cloned.1.call-update) | async-done | bytes 297616 | tf_op jit(solution)/shard_map/psum | solution.py:98
  68.0 1.6 add_add_fusion.3
  69.6 1.0 divide_add_fusion.3
  70.6 0.9 fusion.232
  71.5 0.9 fusion.215
  72.4 0.6 fusion.154
  73.0 0.7 fusion.174
  73.7 1.6 convolution_add_fusion.2
  75.3 0.7 multiply_add_fusion.4
  76.1 1.1 fusion.40
  77.2 1.8 fusion.70
  79.0 0.3 all-reduce.14.cloned.1.call-start
  79.5 47.5 %all-reduce.16.cloned.1.call-done = (f32[2,2,2,100,62]{3,4,2,1,0:T(8,128)}, f32[2,2,100,62]{2,3,1,0:T(8,128)}) async-done(((f32[2,2,2,100,62]{3,4,2,1,0:T(8,128)}, f32[2,2,100,62]{2,3,1,0:T(8,128)}), (f32[2,2,2,100,62]{3,4,2,1,0:T(8,128)}, f32[2,2,100,62]{2,3,1,0:T(8,128)})) %all-reduce.16.cloned.1.call-update) | async-done | bytes 297616 | tf_op jit(solution)/shard_map/psum | solution.py:98
  127.0 1.6 add_add_fusion.2
  128.6 1.0 divide_add_fusion.2
  129.6 0.9 fusion.229
  130.5 0.9 fusion.212
  131.4 0.6 fusion.148
  132.0 0.7 fusion.169
  132.7 1.6 convolution_add_fusion.1
  134.3 0.7 multiply_add_fusion.2
  135.0 1.1 fusion.48
  136.1 1.8 fusion.67
  137.9 0.3 all-reduce.12.cloned.1.call-start
  138.3 0.4 cholesky.18
  138.7 47.3 %all-reduce.14.cloned.1.call-done = (f32[2,2,2,100,62]{3,4,2,1,0:T(8,128)}, f32[2,2,100,62]{2,3,1,0:T(8,128)}) async-done(((f32[2,2,2,100,62]{3,4,2,1,0:T(8,128)}, f32[2,2,100,62]{2,3,1,0:T(8,128)}), (f32[2,2,2,100,62]{3,4,2,1,0:T(8,128)}, f32[2,2,100,62]{2,3,1,0:T(8,128)})) %all-reduce.14.cloned.1.call-update) | async-done | bytes 297616 | tf_op jit(solution)/shard_map/psum | solution.py:98
  186.0 1.5 add_add_fusion.1
  187.5 1.0 divide_add_fusion.1
  188.5 0.9 fusion.226
  189.4 0.9 fusion.209
  190.3 0.6 fusion.142
  190.9 0.7 fusion.164
  191.6 1.6 convolution_add_fusion
  193.2 0.7 multiply_add_fusion
  193.9 1.1 fusion.56
  195.0 1.8 fusion.64
  197.0 0.6 compare_reduce_fusion
  197.6 47.3 %all-reduce.12.cloned.1.call-done = (f32[2,2,2,100,62]{3,4,2,1,0:T(8,128)}, f32[2,2,100,62]{2,3,1,0:T(8,128)}) async-done(((f32[2,2,2,100,62]{3,4,2,1,0:T(8,128)}, f32[2,2,100,62]{2,3,1,0:T(8,128)}), (f32[2,2,2,100,62]{3,4,2,1,0:T(8,128)}, f32[2,2,100,62]{2,3,1,0:T(8,128)})) %all-reduce.12.cloned.1.call-update) | async-done | bytes 297616 | tf_op jit(solution)/shard_map/psum | solution.py:98
  244.9 1.6 add_add_fusion
  246.5 1.0 copy_add_fusion
  247.5 1.2 fusion.202
  248.8 1.1 copy.52
  249.8 0.7 select_select_fusion
  250.5 0.7 fusion.323
  252.5 0.9 copy.56
  253.4 179.1 %all-reduce.10.cloned.1.call-done = f32[4,2,2,100,62]{3,2,4,1,0:T(2,128)} async-done(((f32[4,2,2,100,62]{3,2,4,1,0:T(2,128)}), f32[4,2,2,100,62]{3,2,4,1,0:T(2,128)}) %all-reduce.10.cloned.1.call-update) | async-done | bytes 396816 | tf_op jit(solution)/shard_map/psum | solution.py:109
  432.5 4.9 %fusion.244 = (f32[1,2,2,100,62]{3,2,4,1,0:T(2,128)S(1)}, f32[1,2,2,100,62]{3,2,4,1,0:T(2,128)S(1)}) fusion(f32[4,2,2,100,62]{3,2,4,1,0:T(2,128)} %all-reduce.10.cloned.1.call-done, f32[]{:T(128)} %bitcast.48, f32[]{:T(128)} %bitcast.47, f32[]{:T(128)} %bitcast.46, f32[]{:T(128)} %bitcast.43, f32[]{:T(128)} %bitcast.45, f32[]{:T(128)} %bitcast.44), kind=kLoop, calls=%fused_computation.284 | loop fusion | flops 223200 | bytes 496024 | tf_op jit(solution)/shard_map/div | solution.py:66
  437.3 6.9 %subtract_divide_fusion = (f32[1,2,2,100,62]{3,2,4,1,0:T(2,128)S(1)}, f32[1,2,2,100,62]{3,2,4,1,0:T(2,128)S(1)}, f32[1,2,2,100,62]{3,2,4,1,0:T(2,128)S(1)}, f32[1,2,2,100,62]{3,2,4,1,0:T(2,128)S(1)}) fusion(f32[]{:T(128)} %bitcast.50, f32[]{:T(128)} %bitcast.47, f32[]{:T(128)} %bitcast.44, f32[]{:T(128)} %bitcast.43, ...), kind=kLoop, calls=%fused_computation.288 | loop fusion | flops 570400 | bytes 793640 | tf_op jit(solution)/shard_map/div | solution.py:72
  444.3 0.3 pad_maximum_fusion
  444.5 1.0 fusion.192
  445.6 0.9 copy.58
  446.5 0.9 copy.57
  (35 shorter events, 0.9 us)
Async XLA Ops:
  7.2 3.3 copy-start
  7.2 60.9 %all-reduce.18.cloned.1.call-start = ((), (), s32[]{:S(2)}) async-start(), calls=%async_computation.4 | async-start | bytes 786432 | tf_op jit(solution)/shard_map/psum | solution.py:98
  13.5 1.6 copy-start.2
  17.0 2.1 copy-start.5
  17.0 51.1 %copy-start.4 = (f32[100]{0:T(128)S(1)}, f32[100]{0:T(128)}, u32[]{:S(2)}) copy-start(f32[100]{0:T(128)} %param.16) | copy-start | bytes 1204
  17.0 52.6 %copy-start.1 = (f32[2,2,2,100,62]{3,2,4,1,0:T(2,128)S(1)}, f32[2,2,2,100,62]{3,2,4,1,0:T(2,128)}, u32[]{:S(2)}) copy-start(f32[2,2,2,100,62]{3,2,4,1,0:T(2,128)} %param.15) | copy-start | bytes 595204
  17.0 52.6 %copy-start.3 = (f32[2,2,2,100,62]{3,2,4,1,0:T(2,128)S(1)}, f32[2,2,2,100,62]{3,2,4,1,0:T(2,128)}, u32[]{:S(2)}) copy-start(f32[2,2,2,100,62]{3,2,4,1,0:T(2,128)} %param.14) | copy-start | bytes 595204
  18.8 108.2 %all-reduce.16.cloned.1.call-start = ((), (), s32[]{:S(2)}) async-start(), calls=%async_computation.3 | async-start | bytes 786432 | tf_op jit(solution)/shard_map/psum | solution.py:98
  79.0 107.0 %all-reduce.14.cloned.1.call-start = ((), (), s32[]{:S(2)}) async-start(), calls=%async_computation.2 | async-start | bytes 786432 | tf_op jit(solution)/shard_map/psum | solution.py:98
  137.9 106.9 %all-reduce.12.cloned.1.call-start = ((), (), s32[]{:S(2)}) async-start(), calls=%async_computation.1 | async-start | bytes 786432 | tf_op jit(solution)/shard_map/psum | solution.py:98
  196.8 235.6 %all-reduce.10.cloned.1.call-start = ((), (), s32[]{:S(2)}) async-start(), calls=%async_computation | async-start | bytes 1015808 | tf_op jit(solution)/shard_map/psum | solution.py:109
Sparse Core Ops, SparseCore 0:
  18.9 49.0 all-reduce.17
  79.1 47.8 all-reduce.15
  138.1 47.9 all-reduce.13
  197.0 47.8 all-reduce.11
  250.0 182.4 all-reduce.9
where the time goes:
time: 455 us; the launch traced here: 454 us
  waiting for transfers between devices  370 us (81%)
  other arithmetic  30.3 us (7%)
  matrix products  30.2 us (7%)
  between operations  15.4 us (3%)
  local copies, waits for them, and re-layouts  7.62 us (2%)
    psum x4, waiting for transfers between devices, shards(): numer, curv = lax.psum((numer, curv), 'bl')  190 us
    psum x1, waiting for transfers between devices, shards(): total = lax.psum(partial_value, 'freq')  179 us
    dot_general x16, matrix products, to_stations(): return jnp.einsum('...r,sr->...s', values, one_hot, precision=HIGH)  20.7 us
    add x7, other arithmetic, lm_update(): return gains + (numer - rate * (gains - target)) / (curv + damp + rate)  9.21 us
  transfers between devices with their start and end apart: 5, of which 5 were waited for; matrix products, arithmetic and copies ran while one was open for 1% of the time, Pallas kernels for 0%

commit v1 on v0

v1 whole, which is shorter than its diff:
```python
import functools

import jax
import jax.numpy as jnp
import numpy as np
from jax import lax
from jax.experimental import pallas as pl
from jax.experimental.pallas import tpu as pltpu
from jax.sharding import PartitionSpec as P

MESH = pl.DeviceIdType.MESH
OFFSETS = (0, 1, 3, 2)
HALF = 64
WIDE = 256


def bernstein(position):
    other = 1.0 - position
    return np.stack(
        [
            other * other * other,
            3.0 * position * other * other,
            3.0 * position * position * other,
            position * position * position,
        ],
        axis=-1,
    )


def kernel(
    freqs,
    vis,
    coh,
    pairs,
    flags,
    gains_in,
    cons_in,
    dual_in,
    penalty,
    damping,
    gains_out,
    cons_out,
    dual_out,
    send_coh,
    coh_all,
    send_aux,
    aux_all,
    hot,
    hot_t,
    picked,
    terms,
    sums,
    gains,
    target,
    dual,
    rate,
    table,
    pad,
    gains_all,
    fwd_src,
    fwd_all,
    part_src,
    part_in,
    back_src,
    cons_mine,
    cons_other,
    packed,
    coh_send,
    coh_recv,
    aux_send,
    aux_recv,
    gain_send,
    gain_recv,
    misc,
):
    dirs, stations = gains_in.shape[-2:]
    rows = coh.shape[-1]
    ktiles = gains.shape[0] // 8
    owners, per_owner = fwd_src.shape[:2]
    me = lax.axis_index("freq")
    lane = lax.axis_index("bl")
    group = len(OFFSETS)

    def place(problem):
        return lax.rem(problem, 2), problem // 2

    barrier = pltpu.get_barrier_semaphore()

    def greet(step, carry):
        other = lax.rem(me + step, freqs)
        pl.semaphore_signal(barrier, inc=1, device_id={"freq": other}, device_id_type=MESH)
        return carry

    for off in OFFSETS[1:]:
        other = lax.rem(lane + off, group)
        pl.semaphore_signal(barrier, inc=1, device_id={"bl": other}, device_id_type=MESH)
    lax.fori_loop(1, freqs, greet, 0)

    def fill(off, coh_to, aux_to):
        chan, pol = place(lax.rem(lane + off, group))
        weight = flags[pl.ds(chan, 1), :].astype(jnp.float32)
        for part in range(2):
            base = part * ktiles * 8
            coh_to[base : base + dirs, :] = coh[part, chan, pol].astype(jnp.float32) * weight
            if ktiles * 8 > dirs:
                coh_to[base + dirs : base + ktiles * 8, :] = jnp.zeros((ktiles * 8 - dirs, rows), jnp.float32)
            aux_to[part : part + 1, :] = vis[part, chan, pl.ds(pol, 1), :] * weight
            aux_to[2 + part : 3 + part, :] = pairs[part : part + 1, :].astype(jnp.float32)
        aux_to[4:8, :] = jnp.zeros((4, rows), jnp.float32)

    def coh_copy(slot, off):
        return pltpu.make_async_remote_copy(
            src_ref=send_coh.at[slot - 1],
            dst_ref=coh_all.at[slot],
            send_sem=coh_send.at[slot],
            recv_sem=coh_recv.at[slot],
            device_id={"bl": lax.rem(lane + off, group)},
            device_id_type=MESH,
        )

    def aux_copy(slot, off):
        return pltpu.make_async_remote_copy(
            src_ref=send_aux.at[slot - 1],
            dst_ref=aux_all.at[slot],
            send_sem=aux_send.at[slot],
            recv_sem=aux_recv.at[slot],
            device_id={"bl": lax.rem(lane + off, group)},
            device_id_type=MESH,
        )

    for slot in range(1, group):
        fill(OFFSETS[slot], send_coh.at[slot - 1], send_aux.at[slot - 1])
    pl.semaphore_wait(barrier, freqs - 1 + group - 1)
    for slot in range(1, group):
        aux_copy(slot, OFFSETS[slot]).start()
    for slot in range(1, group):
        coh_copy(slot, OFFSETS[slot]).start()
    fill(0, coh_all.at[0], aux_all.at[0])

    lanes = lax.broadcasted_iota(jnp.int32, (8 * ktiles, 2 * HALF), 1)
    low = lanes < HALF
    chan, pol = place(lane)
    pad[...] = jnp.zeros_like(pad)

    def pack(ref):
        pad[0:dirs, 0:stations] = ref[0, chan, pol]
        real = pad[...]
        pad[0:dirs, 0:stations] = ref[1, chan, pol]
        return real + pltpu.roll(pad[...], HALF, 1)

    start = pack(gains_in)
    mine = pack(dual_in)
    gains[...] = start
    dual[...] = mine
    target[...] = pack(cons_in) - mine
    pad[0:1, 0:dirs] = penalty[...]
    lane_row = lax.broadcasted_iota(jnp.int32, (1, 2 * HALF), 1)
    spread = jnp.broadcast_to(jnp.where(lane_row < dirs, pad[0:1, :], 0.0), (2 * HALF, 2 * HALF))
    rate[...] = spread.T[0 : 8 * ktiles, :]

    def hots(slot):
        ids = lax.broadcasted_iota(jnp.int32, (2 * HALF, rows), 0)
        ids = jnp.where(ids >= HALF, ids - HALF, ids).astype(jnp.float32)
        for part in range(2):
            ones = jnp.where(ids == aux_all[slot, 2 + part : 3 + part, :], 1.0, 0.0)
            hot[slot, :, part * rows : (part + 1) * rows] = ones.astype(jnp.bfloat16)
            hot_t[slot, part * rows : (part + 1) * rows, :] = ones.T.astype(jnp.bfloat16)

    def spread_table():
        value = gains[...]
        high = value.astype(jnp.bfloat16).astype(jnp.float32)
        rest = value - high
        real = jnp.where(low, high, pltpu.roll(rest, HALF, 1))
        imag = jnp.where(low, pltpu.roll(high, HALF, 1), rest)
        for k in range(ktiles):
            both = jnp.concatenate([real[8 * k : 8 * k + 8], imag[8 * k : 8 * k + 8]], axis=0)
            table[16 * k : 16 * k + 16, :] = both.astype(jnp.bfloat16)

    def accumulate(slot):
        picked[...] = jnp.dot(table[...], hot[slot], preferred_element_type=jnp.float32)
        for at in range(0, rows, WIDE):
            first = slice(at, at + WIDE)
            second = slice(rows + at, rows + at + WIDE)

            def load(k):
                cre = coh_all[slot, 8 * k : 8 * k + 8, first]
                cim = coh_all[slot, 8 * (ktiles + k) : 8 * (ktiles + k) + 8, first]
                pre = picked[16 * k : 16 * k + 8, first]
                pim = picked[16 * k + 8 : 16 * k + 16, first]
                qre = picked[16 * k : 16 * k + 8, second]
                qim = picked[16 * k + 8 : 16 * k + 16, second]
                return cre, cim, pre, pim, qre, qim

            mre = jnp.zeros((8, WIDE), jnp.float32)
            mim = jnp.zeros((8, WIDE), jnp.float32)
            for k in range(ktiles):
                cre, cim, pre, pim, qre, qim = load(k)
                tre = cre * qre + cim * qim
                tim = cim * qre - cre * qim
                mre = mre + (pre * tre - pim * tim)
                mim = mim + (pre * tim + pim * tre)
            rre = aux_all[slot, 0:1, first] - jnp.sum(mre, axis=0, keepdims=True)
            rim = aux_all[slot, 1:2, first] - jnp.sum(mim, axis=0, keepdims=True)
            rre = jnp.broadcast_to(rre, (8, WIDE))
            rim = jnp.broadcast_to(rim, (8, WIDE))
            held = [None, None]
            for k in range(ktiles):
                cre, cim, pre, pim, qre, qim = load(k)
                are = rre * cre + rim * cim
                aim = rim * cre - rre * cim
                square = cre * cre + cim * cim
                sides = (
                    (first, are * qre - aim * qim, are * qim + aim * qre, square * (qre * qre + qim * qim)),
                    (second, are * pre + aim * pim, are * pim - aim * pre, square * (pre * pre + pim * pim)),
                )
                for side, (cols, real, imag, curv) in enumerate(sides):
                    both = jnp.concatenate([real, imag], axis=0)
                    high = both.astype(jnp.bfloat16)
                    terms[32 * k : 32 * k + 16, cols] = high
                    terms[32 * k + 16 : 32 * k + 32, cols] = (both - high.astype(jnp.float32)).astype(jnp.bfloat16)
                    base = 32 * ktiles + 8 * (k - k % 2)
                    if k % 2:
                        both = jnp.concatenate([held[side], curv], axis=0)
                        terms[base : base + 16, cols] = both.astype(jnp.bfloat16)
                    elif k == ktiles - 1:
                        both = jnp.concatenate([curv, jnp.zeros_like(curv)], axis=0)
                        terms[base : base + 16, cols] = both.astype(jnp.bfloat16)
                    held[side] = curv
        sums[...] += jnp.dot(terms[...], hot_t[slot], preferred_element_type=jnp.float32)

    def update(damp):
        half = lax.broadcasted_iota(jnp.int32, (8, 2 * HALF), 1) < HALF
        for k in range(ktiles):
            at = slice(8 * k, 8 * k + 8)
            real = sums[32 * k : 32 * k + 8, :] + sums[32 * k + 16 : 32 * k + 24, :]
            imag = sums[32 * k + 8 : 32 * k + 16, :] + sums[32 * k + 24 : 32 * k + 32, :]
            numer = jnp.where(half, real, imag)
            curv = sums[32 * ktiles + 8 * k : 32 * ktiles + 8 * k + 8, :]
            value = gains[at, :]
            pull = rate[at, :]
            gains[at, :] = value + (numer - pull * (value - target[at, :])) / (curv + damp + pull)

    def one_step(step, carry):
        spread_table()
        sums[...] = jnp.zeros_like(sums)

        def one_slot(slot, inner):
            @pl.when(step == 0)
            def _():
                @pl.when(slot > 0)
                def _():
                    aux_copy(slot, 0).wait_recv()
                hots(slot)

                @pl.when(slot > 0)
                def _():
                    coh_copy(slot, 0).wait_recv()

            accumulate(slot)
            return inner

        lax.fori_loop(0, group, one_slot, 0)
        update(damping[step])
        return carry

    lax.fori_loop(0, damping.shape[0], one_step, 0)

    blend = gains[...] + dual[...]
    for owner in range(owners):
        count = min(per_owner, dirs - owner * per_owner)
        fwd_src[owner, 0:count, :] = blend[owner * per_owner : owner * per_owner + count, :]
        if count < per_owner:
            fwd_src[owner, count:per_owner, :] = jnp.zeros((per_owner - count, 2 * HALF), jnp.float32)

    def fwd_copy(other):
        return pltpu.make_async_remote_copy(
            src_ref=fwd_src.at[other],
            dst_ref=fwd_all.at[me],
            send_sem=misc.at[0],
            recv_sem=misc.at[1],
            device_id={"freq": other},
            device_id_type=MESH,
        )

    def send_fwd(step, carry):
        other = lax.rem(me + step, freqs)

        @pl.when(other < owners)
        def _():
            fwd_copy(other).start()

        return carry

    lax.fori_loop(1, freqs, send_fwd, 0)

    def gain_copy(slot, off):
        return pltpu.make_async_remote_copy(
            src_ref=gains,
            dst_ref=gains_all.at[slot],
            send_sem=gain_send.at[slot],
            recv_sem=gain_recv.at[slot],
            device_id={"bl": lax.rem(lane + off, group)},
            device_id_type=MESH,
        )

    for slot in range(1, group):
        gain_copy(slot, OFFSETS[slot]).start()
    gains_all[0] = gains[...]

    def wait_bytes(ref, count, sem):
        view = ref.at[0:count]
        pltpu.make_async_copy(view, view, sem).wait()

    total = 2 * freqs
    basis = bernstein((np.arange(total) + 0.5) / total)
    factor = np.linalg.cholesky(basis.T @ basis)
    is_owner = me < owners

    def part_copy():
        return pltpu.make_async_remote_copy(
            src_ref=part_src,
            dst_ref=part_in,
            send_sem=misc.at[2],
            recv_sem=misc.at[3],
            device_id={"bl": lane + 1 - 2 * lax.rem(lane, 2)},
            device_id_type=MESH,
        )

    def back_copy(other):
        return pltpu.make_async_remote_copy(
            src_ref=back_src.at[other],
            dst_ref=cons_mine.at[me],
            send_sem=misc.at[4],
            recv_sem=misc.at[5],
            device_id={"freq": other},
            device_id_type=MESH,
        )

    @pl.when(is_owner)
    def _():
        fwd_all[me] = fwd_src[me]
        wait_bytes(fwd_all, freqs - 1, misc.at[1])
        for odd in range(2):

            @pl.when(chan == odd)
            def _():
                acc = [None] * 4
                for f in range(freqs):
                    value = fwd_all[f]
                    for m in range(4):
                        term = value * float(basis[2 * f + odd, m])
                        acc[m] = term if acc[m] is None else acc[m] + term
                for m in range(4):
                    part_src[m] = acc[m]

        part_copy().start()
        part_copy().wait_recv()
        whole = [part_src[m] + part_in[m] for m in range(4)]
        forward = []
        for row in range(4):
            acc = whole[row]
            for col in range(row):
                acc = acc - float(factor[row, col]) * forward[col]
            forward.append(acc * float(1.0 / factor[row, row]))
        coeffs = [None] * 4
        for row in range(3, -1, -1):
            acc = forward[row]
            for col in range(row + 1, 4):
                acc = acc - float(factor[col, row]) * coeffs[col]
            coeffs[row] = acc * float(1.0 / factor[row, row])
        for f in range(freqs):
            for odd in range(2):
                value = coeffs[0] * float(basis[2 * f + odd, 0])
                for m in range(1, 4):
                    value = value + coeffs[m] * float(basis[2 * f + odd, m])
                back_src[f, odd] = value

        def send_back(step, carry):
            back_copy(lax.rem(me + step, freqs)).start()
            return carry

        lax.fori_loop(1, freqs, send_back, 0)
        cons_mine[me] = back_src[me]
        wait_bytes(cons_mine, owners - 1, misc.at[5])

    @pl.when(jnp.logical_not(is_owner))
    def _():
        wait_bytes(cons_mine, owners, misc.at[5])

    swap = pltpu.make_async_remote_copy(
        src_ref=cons_mine,
        dst_ref=cons_other,
        send_sem=misc.at[6],
        recv_sem=misc.at[7],
        device_id={"bl": group - 1 - lane},
        device_id_type=MESH,
    )
    swap.start()

    for slot in range(1, group):
        gain_copy(slot, OFFSETS[slot]).wait_recv()

    def unpack(held, index):
        for odd in range(2):
            for owner in range(owners):
                count = min(per_owner, dirs - owner * per_owner)
                at = slice(owner * per_owner, owner * per_owner + count)
                packed[index, odd, at, :] = held[owner, odd, 0:count, :]

    def emit(slot, index):
        problem = lax.rem(lane + group - OFFSETS[slot], group)
        chan_of, pol_of = place(problem)
        solved = gains_all[slot]
        fitted = packed[index, chan_of]
        for part in range(2):
            if part:
                solved = pltpu.roll(solved, HALF, 1)
                fitted = pltpu.roll(fitted, HALF, 1)
            g = solved[0:dirs, 0:stations]
            c = fitted[0:dirs, 0:stations]
            gains_out[part, chan_of, pol_of] = g
            cons_out[part, chan_of, pol_of] = c
            dual_out[part, chan_of, pol_of] = dual_in[part, chan_of, pol_of] + g - c

    unpack(cons_mine, 0)
    emit(0, 0)
    swap.wait_recv()
    unpack(cons_other, 1)
    for slot in range(1, group):
        problem = lax.rem(lane + group - OFFSETS[slot], group)
        emit(slot, jnp.where(problem // 2 == pol, 0, 1))

    for slot in range(1, group):
        coh_copy(slot, OFFSETS[slot]).wait_send()
        aux_copy(slot, OFFSETS[slot]).wait_send()
        gain_copy(slot, OFFSETS[slot]).wait_send()
    swap.wait_send()

    @pl.when(is_owner)
    def _():
        wait_bytes(fwd_src, owners - 1, misc.at[0])
        part_copy().wait_send()
        wait_bytes(back_src, freqs - 1, misc.at[4])

    @pl.when(jnp.logical_not(is_owner))
    def _():
        wait_bytes(fwd_src, owners, misc.at[0])


def solution(mesh):
    freqs = mesh.shape["freq"]

    def step(vis, coh, pairs, flags, gains_in, cons_in, dual_in, penalty, damping):
        dirs = gains_in.shape[-2]
        rows = coh.shape[-1]
        ktiles = -(-dirs // 8)
        krows = 8 * ktiles
        term_rows = 32 * ktiles + 16 * (-(-ktiles // 2))
        group = len(OFFSETS)
        per_owner = -(-dirs // freqs)
        owners = -(-dirs // per_owner)
        lanes = 2 * HALF
        f32, b16 = jnp.float32, jnp.bfloat16
        whole = pl.BlockSpec(memory_space=pltpu.VMEM)
        scratch = [
            pltpu.VMEM((group - 1, 2 * krows, rows), f32),
            pltpu.VMEM((group, 2 * krows, rows), f32),
            pltpu.VMEM((group - 1, 8, rows), f32),
            pltpu.VMEM((group, 8, rows), f32),
            pltpu.VMEM((group, lanes, 2 * rows), b16),
            pltpu.VMEM((group, 2 * rows, lanes), b16),
            pltpu.VMEM((2 * krows, 2 * rows), f32),
            pltpu.VMEM((term_rows, 2 * rows), b16),
            pltpu.VMEM((term_rows, lanes), f32),
            pltpu.VMEM((krows, lanes), f32),
            pltpu.VMEM((krows, lanes), f32),
            pltpu.VMEM((krows, lanes), f32),
            pltpu.VMEM((krows, lanes), f32),
            pltpu.VMEM((2 * krows, lanes), b16),
            pltpu.VMEM((krows, lanes), f32),
            pltpu.VMEM((group, krows, lanes), f32),
            pltpu.VMEM((owners, per_owner, lanes), f32),
            pltpu.VMEM((freqs, per_owner, lanes), f32),
            pltpu.VMEM((4, per_owner, lanes), f32),
            pltpu.VMEM((4, per_owner, lanes), f32),
            pltpu.VMEM((freqs, 2, per_owner, lanes), f32),
            pltpu.VMEM((owners, 2, per_owner, lanes), f32),
            pltpu.VMEM((owners, 2, per_owner, lanes), f32),
            pltpu.VMEM((2, 2, krows, lanes), f32),
        ] + [pltpu.SemaphoreType.DMA((n,)) for n in (group, group, group, group, group, group, 8)]
        out = jax.ShapeDtypeStruct(gains_in.shape, f32)
        return pl.pallas_call(
            functools.partial(kernel, freqs),
            out_shape=(out, out, out),
            in_specs=[whole] * 8 + [pl.BlockSpec(memory_space=pltpu.SMEM)],
            out_specs=(whole, whole, whole),
            scratch_shapes=scratch,
            compiler_params=pltpu.CompilerParams(
                collective_id=0, has_side_effects=True, vmem_limit_bytes=40 * 1024 * 1024
            ),
        )(vis, coh, pairs, flags, gains_in, cons_in, dual_in, penalty.reshape(1, dirs), damping)

    spread = P(None, "freq", None, None, None)
    return jax.shard_map(
        step,
        mesh=mesh,
        in_specs=(
            P(None, "freq", None, "bl"),
            P(None, "freq", None, None, "bl"),
            P(None, "bl"),
            P("freq", "bl"),
            spread,
            spread,
            spread,
            P(),
            P(),
        ),
        out_specs=(spread, spread, spread),
        check_vma=False,
    )
```

time: 455 us -> 72.2 us (0.16)
  waiting for transfers between devices: 370 us -> 0 us
  Pallas kernels: 0 us -> 65.6 us
  other arithmetic: 30.3 us -> 0 us
  matrix products: 30.2 us -> 0 us
  between operations: 15.4 us -> 0.69 us
    psum x5 -> x0, waiting for transfers between devices: 370 us -> none  [the longest x4 190 us: shards(): numer, curv = lax.psum((numer, curv), 'bl')]
    pallas_call x0 -> x1, Pallas kernels: none -> 65.6 us  [step(): pl.pallas_call(functools.partial(kernel, freqs), out_shape=(out, out, out...]
    dot_general x27 -> x0, matrix products: 30.2 us -> none  [the longest x16 20.7 us: to_stations(): return jnp.einsum('...r,sr->...s', values, one_hot, precision=HIGH)]
    add x12 -> x0, other arithmetic: 13.2 us -> none  [the longest x7 9.21 us: lm_update(): return gains + (numer - rate * (gains - target)) / (curv + damp + rate)]
    div x3 -> x0, other arithmetic: 11.8 us -> none  [the longest x1 6.93 us: fit_coeffs(): backward[row] = acc / factor[row, row]]
  transfers between devices with their start and end apart: 5 -> 0, of which waited for: 5 -> 0; matrix products, arithmetic and copies ran while one was open for 1% -> 0% of each run, Pallas kernels for 0% -> 0%
where the time goes in v1:
time: 72.2 us; the launch traced here: 72 us
  Pallas kernels  65.6 us (91%)
  local copies, waits for them, and re-layouts  5.74 us (8%)
    pallas_call x1, Pallas kernels, step(): pl.pallas_call(functools.partial(kernel, freqs), out_shape=(out, out, out...  65.6 us
    unnamed x20, local copies, waits for them, and re-layouts  3.07 us
    pallas_call x3, local copies, waits for them, and re-layouts, step(): pl.pallas_call(functools.partial(kernel, freqs), out_shape=(out, out, out...  2.67 us

profile of v1, /device:TPU:1, one launch (start us, length us, event | category | flops | bytes accessed | tf_op | source)
XLA Modules:
  0.0 72.0 jit_solution(13461113802487236853)
XLA Ops:
  0.6 0.0 copy-start.6
  0.6 0.0 copy-start.7
  0.7 1.2 %copy.13.gains_in = f32[2,2,2,100,62]{4,3,2,1,0:T(8,128)S(1)} copy(f32[2,2,2,100,62]{3,2,4,1,0:T(2,128)} %param.13) | data formatting | bytes 396800 | tf_op args[4]
  1.9 0.0 copy-done.6
  1.9 0.0 copy-start.5
  1.9 0.2 copy.14.cons_in
  2.1 0.0 copy-done.7
  2.1 0.2 copy.15.dual_in
  2.3 0.7 copy-done.5
  3.0 0.0 copy-start
  3.0 0.0 copy-start.1
  3.0 0.0 copy-start.2
  3.0 0.0 copy-start.3
  3.0 0.0 copy-start.4
  3.0 0.1 copy.12.coh
  3.2 0.6 copy-done
  3.7 0.0 copy-done.1
  3.7 0.0 copy-done.2
  3.7 0.0 copy-done.3
  3.8 0.0 copy-done.4
  3.8 65.6 %shard_map.112 = (f32[2,2,2,100,62]{4,3,2,1,0:T(8,128)S(1)}, f32[2,2,2,100,62]{4,3,2,1,0:T(8,128)S(1)}, f32[2,2,2,100,62]{4,3,2,1,0:T(8,128)S(1)}) custom-call(f32[2,2,2,512]{3,2,1,0:T(2,128)S(1)} %copy-done, bf16[2,2,2,100,512]{4,3,2,1,0:T(8,128)(2,1)S(1)} %copy.12.coh, s32[2,512]{1,0:T(2,128)S(1)} %copy-done.1, s32[2,512]{1,0:T(2,128)S(1)} %copy-done.2, ...), custom_call_target="tpu_custom_call" | custom-call | tf_op jit(solution)/shard_map/pallas_call | solution.py:492
  69.4 0.9 %copy.16 = f32[2,2,2,100,62]{3,2,4,1,0:T(2,128)} copy(f32[2,2,2,100,62]{4,3,2,1,0:T(8,128)S(1)} %get-tuple-element.3) | data formatting | bytes 396800 | tf_op jit(solution)/shard_map/pallas_call | solution.py:492
  70.3 0.9 %copy.17 = f32[2,2,2,100,62]{3,2,4,1,0:T(2,128)} copy(f32[2,2,2,100,62]{4,3,2,1,0:T(8,128)S(1)} %get-tuple-element.4) | data formatting | bytes 396800 | tf_op jit(solution)/shard_map/pallas_call | solution.py:492
  71.1 0.9 %copy.18 = f32[2,2,2,100,62]{3,2,4,1,0:T(2,128)} copy(f32[2,2,2,100,62]{4,3,2,1,0:T(8,128)S(1)} %get-tuple-element.5) | data formatting | bytes 396800 | tf_op jit(solution)/shard_map/pallas_call | solution.py:492
Async XLA Ops:
  0.6 1.2 %copy-start.6 = (f32[2,2,2,100,62]{3,2,4,1,0:T(2,128)S(1)}, f32[2,2,2,100,62]{3,2,4,1,0:T(2,128)}, u32[]{:S(2)}) copy-start(f32[2,2,2,100,62]{3,2,4,1,0:T(2,128)} %param.14) | copy-start | bytes 595204
  0.6 1.5 %copy-start.7 = (f32[2,2,2,100,62]{3,2,4,1,0:T(2,128)S(1)}, f32[2,2,2,100,62]{3,2,4,1,0:T(2,128)}, u32[]{:S(2)}) copy-start(f32[2,2,2,100,62]{3,2,4,1,0:T(2,128)} %param.15) | copy-start | bytes 595204
  1.9 1.2 %copy-start.5 = (bf16[2,2,2,100,512]{4,2,3,1,0:T(2,128)(2,1)S(1)}, bf16[2,2,2,100,512]{4,2,3,1,0:T(2,128)(2,1)}, u32[]{:S(2)}) copy-start(bf16[2,2,2,100,512]{4,2,3,1,0:T(2,128)(2,1)} %param.10) | copy-start | bytes 2457604
  3.0 0.7 copy-start
  3.0 0.7 copy-start.1
  3.0 0.7 copy-start.2
  3.0 0.7 copy-start.3
  3.0 0.7 copy-start.4

commit v2 on v1

v2 whole, which is shorter than its diff:
```python
import functools

import jax
import jax.numpy as jnp
import numpy as np
from jax import lax
from jax.experimental import pallas as pl
from jax.experimental.pallas import tpu as pltpu
from jax.sharding import PartitionSpec as P

MESH = pl.DeviceIdType.MESH
OFFSETS = (0, 1, 3, 2)
HALF = 64
WIDE = 256


def bernstein(position):
    other = 1.0 - position
    return np.stack(
        [
            other * other * other,
            3.0 * position * other * other,
            3.0 * position * position * other,
            position * position * position,
        ],
        axis=-1,
    )


def kernel(
    freqs,
    vis,
    coh,
    pairs,
    flags,
    gains_in,
    cons_in,
    dual_in,
    penalty,
    damping,
    gains_out,
    cons_out,
    dual_out,
    send_coh,
    coh_all,
    send_aux,
    aux_all,
    hot,
    hot_t,
    picked,
    terms,
    sums,
    gains,
    target,
    dual,
    rate,
    table,
    pad,
    gains_all,
    fwd_src,
    fwd_all,
    part_src,
    part_in,
    back_src,
    cons_all,
    coh_send,
    coh_recv,
    aux_send,
    aux_recv,
    gain_send,
    gain_recv,
    back_recv,
    misc,
):
    stations, dirs = gains_in.shape[2], gains_in.shape[4]
    rows = coh.shape[-1]
    ktiles = gains.shape[0] // 8
    per_owner = HALF // freqs
    plane = min(8, freqs)
    planes = freqs // plane
    even = dirs // 8 * 8
    rest = dirs - even
    me = lax.axis_index("freq")
    lane = lax.axis_index("bl")
    group = len(OFFSETS)

    def place(problem):
        return lax.rem(problem, 2), problem // 2

    barrier = pltpu.get_barrier_semaphore()

    def greet(step, carry):
        other = lax.rem(me + step, freqs)
        pl.semaphore_signal(barrier, inc=1, device_id={"freq": other}, device_id_type=MESH)
        return carry

    for off in OFFSETS[1:]:
        other = lax.rem(lane + off, group)
        pl.semaphore_signal(barrier, inc=1, device_id={"bl": other}, device_id_type=MESH)
    lax.fori_loop(1, freqs, greet, 0)

    def fill(off, coh_to, aux_to):
        chan, pol = place(lax.rem(lane + off, group))
        weight = flags[pl.ds(chan, 1), :].astype(jnp.float32)
        for part in range(2):
            value = coh[part, chan, pol].astype(jnp.float32) * weight
            coh_to[part * even : (part + 1) * even, :] = value[0:even]
            coh_to[2 * even + part * rest : 2 * even + (part + 1) * rest, :] = value[even:dirs]
            aux_to[part : part + 1, :] = vis[part, chan, pl.ds(pol, 1), :] * weight
            aux_to[2 + part : 3 + part, :] = pairs[part : part + 1, :].astype(jnp.float32)

    def coh_copy(slot, off):
        return pltpu.make_async_remote_copy(
            src_ref=send_coh.at[slot - 1],
            dst_ref=coh_all.at[slot],
            send_sem=coh_send.at[slot],
            recv_sem=coh_recv.at[slot],
            device_id={"bl": lax.rem(lane + off, group)},
            device_id_type=MESH,
        )

    def aux_copy(slot, off):
        return pltpu.make_async_remote_copy(
            src_ref=send_aux.at[slot - 1],
            dst_ref=aux_all.at[slot],
            send_sem=aux_send.at[slot],
            recv_sem=aux_recv.at[slot],
            device_id={"bl": lax.rem(lane + off, group)},
            device_id_type=MESH,
        )

    for slot in range(1, group):
        fill(OFFSETS[slot], send_coh.at[slot - 1], send_aux.at[slot - 1])
    pl.semaphore_wait(barrier, freqs - 1 + group - 1)
    for slot in range(1, group):
        aux_copy(slot, OFFSETS[slot]).start()
    for slot in range(1, group):
        coh_copy(slot, OFFSETS[slot]).start()
    fill(0, coh_all.at[0], aux_all.at[0])

    lanes = lax.broadcasted_iota(jnp.int32, (8 * ktiles, 2 * HALF), 1)
    low = lanes < HALF
    chan, pol = place(lane)

    def pack(ref, to):
        to[...] = jnp.zeros_like(to)
        for part in range(2):
            for n in range(stations):
                to[part * HALF + n : part * HALF + n + 1, 0:dirs] = ref[part, chan, n, pl.ds(pol, 1), :]

    pack(gains_in, pad)
    gains[...] = pad[...].T[0 : 8 * ktiles, :]
    pack(dual_in, dual)
    pack(cons_in, pad)
    target[...] = (pad[...] - dual[...]).T[0 : 8 * ktiles, :]
    pad[...] = jnp.zeros_like(pad)
    pad[0:1, 0:dirs] = penalty[...]
    rate[...] = jnp.broadcast_to(pad[0:1, :], (2 * HALF, 2 * HALF)).T[0 : 8 * ktiles, :]

    def hots(slot):
        ids = lax.broadcasted_iota(jnp.int32, (2 * HALF, rows), 0)
        ids = jnp.where(ids >= HALF, ids - HALF, ids).astype(jnp.float32)
        for part in range(2):
            ones = jnp.where(ids == aux_all[slot, 2 + part : 3 + part, :], 1.0, 0.0)
            hot[slot, :, part * rows : (part + 1) * rows] = ones.astype(jnp.bfloat16)
            hot_t[slot, part * rows : (part + 1) * rows, :] = ones.T.astype(jnp.bfloat16)

    def spread_table():
        value = gains[...]
        high = value.astype(jnp.bfloat16).astype(jnp.float32)
        rest = value - high
        real = jnp.where(low, high, pltpu.roll(rest, HALF, 1))
        imag = jnp.where(low, pltpu.roll(high, HALF, 1), rest)
        for k in range(ktiles):
            both = jnp.concatenate([real[8 * k : 8 * k + 8], imag[8 * k : 8 * k + 8]], axis=0)
            table[16 * k : 16 * k + 16, :] = both.astype(jnp.bfloat16)

    def gather(slot):
        picked[slot] = jnp.dot(table[...], hot[slot], preferred_element_type=jnp.float32)

    def vector(slot):
        for at in range(0, rows, WIDE):
            first = slice(at, at + WIDE)
            second = slice(rows + at, rows + at + WIDE)

            def load(k):
                if 8 * k < even:
                    cre = coh_all[slot, 8 * k : 8 * k + 8, first]
                    cim = coh_all[slot, even + 8 * k : even + 8 * k + 8, first]
                else:
                    cre = coh_all[slot, 2 * even : 2 * even + 8, first]
                    cim = pltpu.roll(cre, rest, 0)
                pre = picked[slot, 16 * k : 16 * k + 8, first]
                pim = picked[slot, 16 * k + 8 : 16 * k + 16, first]
                qre = picked[slot, 16 * k : 16 * k + 8, second]
                qim = picked[slot, 16 * k + 8 : 16 * k + 16, second]
                return cre, cim, pre, pim, qre, qim

            mre = jnp.zeros((8, WIDE), jnp.float32)
            mim = jnp.zeros((8, WIDE), jnp.float32)
            for k in range(ktiles):
                cre, cim, pre, pim, qre, qim = load(k)
                tre = cre * qre + cim * qim
                tim = cim * qre - cre * qim
                mre = mre + (pre * tre - pim * tim)
                mim = mim + (pre * tim + pim * tre)
            rre = aux_all[slot, 0:1, first] - jnp.sum(mre, axis=0, keepdims=True)
            rim = aux_all[slot, 1:2, first] - jnp.sum(mim, axis=0, keepdims=True)
            rre = jnp.broadcast_to(rre, (8, WIDE))
            rim = jnp.broadcast_to(rim, (8, WIDE))
            held = [None, None]
            for k in range(ktiles):
                cre, cim, pre, pim, qre, qim = load(k)
                are = rre * cre + rim * cim
                aim = rim * cre - rre * cim
                square = cre * cre + cim * cim
                sides = (
                    (first, are * qre - aim * qim, are * qim + aim * qre, square * (qre * qre + qim * qim)),
                    (second, are * pre + aim * pim, are * pim - aim * pre, square * (pre * pre + pim * pim)),
                )
                for side, (cols, real, imag, curv) in enumerate(sides):
                    both = jnp.concatenate([real, imag], axis=0)
                    high = both.astype(jnp.bfloat16)
                    terms[slot, 32 * k : 32 * k + 16, cols] = high
                    terms[slot, 32 * k + 16 : 32 * k + 32, cols] = (both - high.astype(jnp.float32)).astype(jnp.bfloat16)
                    base = 32 * ktiles + 8 * (k - k % 2)
                    if k % 2:
                        both = jnp.concatenate([held[side], curv], axis=0)
                        terms[slot, base : base + 16, cols] = both.astype(jnp.bfloat16)
                    elif k == ktiles - 1:
                        both = jnp.concatenate([curv, jnp.zeros_like(curv)], axis=0)
                        terms[slot, base : base + 16, cols] = both.astype(jnp.bfloat16)
                    held[side] = curv

    def scatter(slot):
        sums[...] += jnp.dot(terms[slot], hot_t[slot], preferred_element_type=jnp.float32)

    def update(damp):
        half = lax.broadcasted_iota(jnp.int32, (8, 2 * HALF), 1) < HALF
        for k in range(ktiles):
            at = slice(8 * k, 8 * k + 8)
            real = sums[32 * k : 32 * k + 8, :] + sums[32 * k + 16 : 32 * k + 24, :]
            imag = sums[32 * k + 8 : 32 * k + 16, :] + sums[32 * k + 24 : 32 * k + 32, :]
            numer = jnp.where(half, real, imag)
            curv = sums[32 * ktiles + 8 * k : 32 * ktiles + 8 * k + 8, :]
            value = gains[at, :]
            pull = rate[at, :]
            gains[at, :] = value + (numer - pull * (value - target[at, :])) / (curv + damp + pull)

    def one_step(step, carry):
        spread_table()
        sums[...] = jnp.zeros_like(sums)
        for slot in range(group):
            gather(slot)
        for slot in range(group):
            vector(slot)
            scatter(slot)
        update(damping[step])
        return carry

    spread_table()
    sums[...] = jnp.zeros_like(sums)
    for slot in range(group):
        if slot:
            aux_copy(slot, 0).wait_recv()
        hots(slot)
        gather(slot)
        if slot:
            coh_copy(slot, 0).wait_recv()
        vector(slot)
        scatter(slot)
    update(damping[0])
    lax.fori_loop(1, damping.shape[0], one_step, 0)

    pad[0 : 8 * ktiles, :] = gains[...]
    pad[8 * ktiles : 2 * HALF, :] = jnp.zeros((2 * HALF - 8 * ktiles, 2 * HALF), jnp.float32)
    solved = pad[...].T
    gains_all[lane] = solved
    blend = solved + dual[...]
    for owner in range(freqs):
        for part in range(2):
            base = part * HALF + owner * per_owner
            fwd_src[owner, part * per_owner : (part + 1) * per_owner, :] = blend[base : base + per_owner, :]

    def far_first(send):
        here = me // plane
        order = sorted(range(planes), key=lambda d: -min(d, planes - d))
        for ahead in order:
            base = lax.rem(here + ahead, planes) * plane

            def one(step, carry):
                send(base + lax.rem(me + step, plane))
                return carry

            lax.fori_loop(0 if ahead else 1, plane, one, 0)

    def fwd_copy(other):
        return pltpu.make_async_remote_copy(
            src_ref=fwd_src.at[other],
            dst_ref=fwd_all.at[me],
            send_sem=misc.at[0],
            recv_sem=misc.at[1],
            device_id={"freq": other},
            device_id_type=MESH,
        )

    far_first(lambda other: fwd_copy(other).start())

    def gain_copy(slot, off):
        return pltpu.make_async_remote_copy(
            src_ref=gains_all.at[lane],
            dst_ref=gains_all.at[lane],
            send_sem=gain_send.at[slot],
            recv_sem=gain_recv.at[slot],
            device_id={"bl": lax.rem(lane + off, group)},
            device_id_type=MESH,
        )

    for slot in range(1, group):
        gain_copy(slot, OFFSETS[slot]).start()

    def wait_bytes(ref, count, sem):
        view = ref.at[0:count]
        pltpu.make_async_copy(view, view, sem).wait()

    total = 2 * freqs
    basis = bernstein((np.arange(total) + 0.5) / total)
    factor = np.linalg.cholesky(basis.T @ basis)

    def part_copy():
        return pltpu.make_async_remote_copy(
            src_ref=part_src,
            dst_ref=part_in,
            send_sem=misc.at[2],
            recv_sem=misc.at[3],
            device_id={"bl": lane + 1 - 2 * lax.rem(lane, 2)},
            device_id_type=MESH,
        )

    def back_copy(other):
        return pltpu.make_async_remote_copy(
            src_ref=back_src.at[other],
            dst_ref=cons_all.at[pol, me],
            send_sem=misc.at[4],
            recv_sem=back_recv.at[me // plane],
            device_id={"freq": other},
            device_id_type=MESH,
        )

    def swap_copy(base):
        view = cons_all.at[pol, pl.ds(base, plane)]
        return pltpu.make_async_remote_copy(
            src_ref=view,
            dst_ref=view,
            send_sem=misc.at[5],
            recv_sem=misc.at[6],
            device_id={"bl": group - 1 - lane},
            device_id_type=MESH,
        )

    fwd_all[me] = fwd_src[me]
    wait_bytes(fwd_all, freqs - 1, misc.at[1])
    for odd in range(2):

        @pl.when(chan == odd)
        def _():
            acc = [None] * 4
            for f in range(freqs):
                value = fwd_all[f]
                for m in range(4):
                    term = value * float(basis[2 * f + odd, m])
                    acc[m] = term if acc[m] is None else acc[m] + term
            for m in range(4):
                part_src[m] = acc[m]

    part_copy().start()
    part_copy().wait_recv()
    whole = [part_src[m] + part_in[m] for m in range(4)]
    forward = []
    for row in range(4):
        acc = whole[row]
        for col in range(row):
            acc = acc - float(factor[row, col]) * forward[col]
        forward.append(acc * float(1.0 / factor[row, row]))
    coeffs = [None] * 4
    for row in range(3, -1, -1):
        acc = forward[row]
        for col in range(row + 1, 4):
            acc = acc - float(factor[col, row]) * coeffs[col]
        coeffs[row] = acc * float(1.0 / factor[row, row])
    for f in range(freqs):
        for odd in range(2):
            value = coeffs[0] * float(basis[2 * f + odd, 0])
            for m in range(1, 4):
                value = value + coeffs[m] * float(basis[2 * f + odd, m])
            back_src[f, odd] = value
    far_first(lambda other: back_copy(other).start())
    cons_all[pol, me] = back_src[me]

    def tiles(take):
        for part in range(2):
            for odd in range(2):
                for n in range(stations):
                    take(part, odd, n, n // per_owner, part * per_owner + n % per_owner)

    for slot in range(1, group):
        gain_copy(slot, OFFSETS[slot]).wait_recv()

    def emit_gains(part, odd, n, owner, row):
        at = part * HALF + n
        tile = jnp.concatenate([gains_all[odd, at : at + 1, 0:dirs], gains_all[2 + odd, at : at + 1, 0:dirs]], axis=0)
        gains_out[part, odd, n] = tile
        dual_out[part, odd, n] = dual_in[part, odd, n] + tile

    tiles(emit_gains)

    here = me // plane
    for ahead in sorted(range(planes), key=lambda d: min(d, planes - d)):
        from_plane = lax.rem(here + ahead, planes)
        count = plane if ahead else plane - 1
        view = cons_all.at[pol, pl.ds(from_plane * plane, count)]
        pltpu.make_async_copy(view, view, back_recv.at[from_plane]).wait()
        swap_copy(from_plane * plane).start()
    wait_bytes(cons_all.at[1 - pol], freqs, misc.at[6])

    def emit_cons(part, odd, n, owner, row):
        tile = jnp.concatenate(
            [cons_all[0, owner, odd, row : row + 1, 0:dirs], cons_all[1, owner, odd, row : row + 1, 0:dirs]], axis=0
        )
        cons_out[part, odd, n] = tile
        dual_out[part, odd, n] = dual_out[part, odd, n] - tile

    tiles(emit_cons)

    for slot in range(1, group):
        coh_copy(slot, OFFSETS[slot]).wait_send()
        aux_copy(slot, OFFSETS[slot]).wait_send()
        gain_copy(slot, OFFSETS[slot]).wait_send()
    wait_bytes(fwd_src, freqs - 1, misc.at[0])
    part_copy().wait_send()
    wait_bytes(back_src, freqs - 1, misc.at[4])
    wait_bytes(cons_all.at[pol], freqs, misc.at[5])


def solution(mesh):
    freqs = mesh.shape["freq"]

    def step(vis, coh, pairs, flags, gains_in, cons_in, dual_in, penalty, damping):
        dirs = gains_in.shape[-2]
        rows = coh.shape[-1]
        ktiles = -(-dirs // 8)
        krows = 8 * ktiles
        term_rows = 32 * ktiles + 16 * (-(-ktiles // 2))
        group = len(OFFSETS)
        per_owner = HALF // freqs
        planes = freqs // min(8, freqs)
        lanes = 2 * HALF
        f32, b16 = jnp.float32, jnp.bfloat16
        whole = pl.BlockSpec(memory_space=pltpu.VMEM)
        scratch = [
            pltpu.VMEM((group - 1, 2 * dirs, rows), f32),
            pltpu.VMEM((group, 2 * dirs, rows), f32),
            pltpu.VMEM((group - 1, 4, rows), f32),
            pltpu.VMEM((group, 4, rows), f32),
            pltpu.VMEM((group, lanes, 2 * rows), b16),
            pltpu.VMEM((group, 2 * rows, lanes), b16),
            pltpu.VMEM((group, 2 * krows, 2 * rows), f32),
            pltpu.VMEM((group, term_rows, 2 * rows), b16),
            pltpu.VMEM((term_rows, lanes), f32),
            pltpu.VMEM((krows, lanes), f32),
            pltpu.VMEM((krows, lanes), f32),
            pltpu.VMEM((lanes, lanes), f32),
            pltpu.VMEM((krows, lanes), f32),
            pltpu.VMEM((2 * krows, lanes), b16),
            pltpu.VMEM((lanes, lanes), f32),
            pltpu.VMEM((group, lanes, lanes), f32),
            pltpu.VMEM((freqs, 2 * per_owner, lanes), f32),
            pltpu.VMEM((freqs, 2 * per_owner, lanes), f32),
            pltpu.VMEM((4, 2 * per_owner, lanes), f32),
            pltpu.VMEM((4, 2 * per_owner, lanes), f32),
            pltpu.VMEM((freqs, 2, 2 * per_owner, lanes), f32),
            pltpu.VMEM((2, freqs, 2, 2 * per_owner, lanes), f32),
        ] + [pltpu.SemaphoreType.DMA((n,)) for n in (group,) * 6 + (planes, 8)]

        def turn(value):
            return jnp.transpose(value, (0, 1, 4, 2, 3))

        gains_in, cons_in, dual_in = turn(gains_in), turn(cons_in), turn(dual_in)
        out = jax.ShapeDtypeStruct(gains_in.shape, f32)
        outs = pl.pallas_call(
            functools.partial(kernel, freqs),
            out_shape=(out, out, out),
            in_specs=[whole] * 8 + [pl.BlockSpec(memory_space=pltpu.SMEM)],
            out_specs=(whole, whole, whole),
            scratch_shapes=scratch,
            compiler_params=pltpu.CompilerParams(
                collective_id=0, has_side_effects=True, vmem_limit_bytes=40 * 1024 * 1024
            ),
        )(vis, coh, pairs, flags, gains_in, cons_in, dual_in, penalty.reshape(1, dirs), damping)
        return tuple(jnp.transpose(value, (0, 1, 3, 4, 2)) for value in outs)

    spread = P(None, "freq", None, None, None)
    return jax.shard_map(
        step,
        mesh=mesh,
        in_specs=(
            P(None, "freq", None, "bl"),
            P(None, "freq", None, None, "bl"),
            P(None, "bl"),
            P("freq", "bl"),
            spread,
            spread,
            spread,
            P(),
            P(),
        ),
        out_specs=(spread, spread, spread),
        check_vma=False,
    )
```

time: 72.2 us -> 64 us (0.89)
  Pallas kernels: 65.6 us -> 59.6 us
  local copies, waits for them, and re-layouts: 5.74 us -> 3.52 us
    pallas_call x1, Pallas kernels: 65.6 us -> 59.6 us  [step(): pl.pallas_call(functools.partial(kernel, freqs), out_shape=(out, out, out...]
    pallas_call x3 -> x0, local copies, waits for them, and re-layouts: 2.67 us -> none  [step(): pl.pallas_call(functools.partial(kernel, freqs), out_shape=(out, out, out...]
where the time goes in v2:
time: 64 us; the launch traced here: 63.9 us
  Pallas kernels  59.6 us (93%)
  local copies, waits for them, and re-layouts  3.52 us (6%)
  between operations  0.78 us (1%)
    pallas_call x1, Pallas kernels, step(): pl.pallas_call(functools.partial(kernel, freqs), out_shape=(out, out, out...  59.6 us
    unnamed x20, local copies, waits for them, and re-layouts  3.52 us

profile of v2, /device:TPU:1, one launch (start us, length us, event | category | flops | bytes accessed | tf_op | source)
XLA Modules:
  0.0 63.9 jit_solution(5276275369563164680)
XLA Ops:
  0.6 0.0 copy-start
  0.6 0.0 copy-start.1
  0.7 0.0 copy-start.2
  0.7 0.0 copy-start.3
  0.7 0.0 copy-start.4
  0.7 0.0 copy-start.5
  0.7 0.0 copy-start.6
  0.7 0.0 copy-start.7
  0.7 1.4 %copy.12.coh = bf16[2,2,2,100,512]{4,3,2,1,0:T(8,128)(2,1)S(1)} copy(bf16[2,2,2,100,512]{4,2,3,1,0:T(2,128)(2,1)} %param.10) | data formatting | bytes 1638400 | tf_op args[1]
  2.1 0.0 copy-done
  2.1 0.0 copy-done.1
  2.1 0.0 copy-done.2
  2.1 0.0 copy-done.3
  2.2 0.0 copy-done.4
  2.2 0.0 copy-done.5
  2.2 0.0 copy-done.6
  2.2 0.0 copy-done.7
  2.2 59.6 %shard_map.112 = (f32[2,2,62,2,100]{4,3,2,1,0:T(2,128)S(1)}, f32[2,2,62,2,100]{4,3,2,1,0:T(2,128)S(1)}, f32[2,2,62,2,100]{4,3,2,1,0:T(2,128)S(1)}) custom-call(f32[2,2,2,512]{3,2,1,0:T(2,128)S(1)} %copy-done.3, bf16[2,2,2,100,512]{4,3,2,1,0:T(8,128)(2,1)S(1)} %copy.12.coh, s32[2,512]{1,0:T(2,128)S(1)} %copy-done.4, s32[2,512]{1,0:T(2,128)S(1)} %copy-done.5, ...), custom_call_target="tpu_custom_call" | custom-call | tf_op jit(solution)/shard_map/pallas_call | solution.py:490
  61.8 0.7 %copy.16 = f32[2,2,2,100,62]{3,2,4,1,0:T(2,128)} copy(f32[2,2,2,100,62]{3,2,4,1,0:T(2,128)S(1)} %bitcast.12) | data formatting | bytes 396800
  62.5 0.7 %copy.17 = f32[2,2,2,100,62]{3,2,4,1,0:T(2,128)} copy(f32[2,2,2,100,62]{3,2,4,1,0:T(2,128)S(1)} %bitcast.11) | data formatting | bytes 396800
  63.2 0.7 %copy.18 = f32[2,2,2,100,62]{3,2,4,1,0:T(2,128)} copy(f32[2,2,2,100,62]{3,2,4,1,0:T(2,128)S(1)} %bitcast.10) | data formatting | bytes 396800
Async XLA Ops:
  0.6 1.5 %copy-start = (f32[2,2,2,100,62]{3,2,4,1,0:T(2,128)S(1)}, f32[2,2,2,100,62]{3,2,4,1,0:T(2,128)}, u32[]{:S(2)}) copy-start(f32[2,2,2,100,62]{3,2,4,1,0:T(2,128)} %param.13) | copy-start | bytes 595204
  0.6 1.5 %copy-start.1 = (f32[2,2,2,100,62]{3,2,4,1,0:T(2,128)S(1)}, f32[2,2,2,100,62]{3,2,4,1,0:T(2,128)}, u32[]{:S(2)}) copy-start(f32[2,2,2,100,62]{3,2,4,1,0:T(2,128)} %param.14) | copy-start | bytes 595204
  0.7 1.5 %copy-start.2 = (f32[2,2,2,100,62]{3,2,4,1,0:T(2,128)S(1)}, f32[2,2,2,100,62]{3,2,4,1,0:T(2,128)}, u32[]{:S(2)}) copy-start(f32[2,2,2,100,62]{3,2,4,1,0:T(2,128)} %param.15) | copy-start | bytes 595204
  0.7 1.5 %copy-start.3 = (f32[2,2,2,512]{3,2,1,0:T(2,128)S(1)}, f32[2,2,2,512]{3,2,1,0:T(2,128)}, u32[]{:S(2)}) copy-start(f32[2,2,2,512]{3,2,1,0:T(2,128)} %vis.1) | copy-start | bytes 49156
  0.7 1.5 %copy-start.4 = (s32[2,512]{1,0:T(2,128)S(1)}, s32[2,512]{1,0:T(2,128)}, u32[]{:S(2)}) copy-start(s32[2,512]{1,0:T(2,128)} %pairs.1) | copy-start | bytes 12292
  0.7 1.5 %copy-start.5 = (s32[2,512]{1,0:T(2,128)S(1)}, s32[2,512]{1,0:T(2,128)}, u32[]{:S(2)}) copy-start(s32[2,512]{1,0:T(2,128)} %flags.1) | copy-start | bytes 12292
  0.7 1.5 %copy-start.6 = (f32[100]{0:T(128)S(1)}, f32[100]{0:T(128)}, u32[]{:S(2)}) copy-start(f32[100]{0:T(128)} %param.16) | copy-start | bytes 1204
  0.7 1.5 %copy-start.7 = (f32[4]{0:T(128)S(1)}, f32[4]{0:T(128)}, u32[]{:S(2)}) copy-start(f32[4]{0:T(128)} %damping.1) | copy-start | bytes 52

commit v3 on v2

--- a/solution.py
+++ b/solution.py
@@ -71,6 +71,7 @@
     gain_recv,
     back_recv,
     misc,
+    rounds,
 ):
     stations, dirs = gains_in.shape[2], gains_in.shape[4]
     rows = coh.shape[-1]
@@ -87,17 +88,33 @@
     def place(problem):
         return lax.rem(problem, 2), problem // 2
 
+    deep = max(1, freqs // 8)
+    wide = freqs // (2 * deep)
+
+    def freq_at(dz, dy, dc):
+        z = lax.rem(me // (2 * wide) + dz, deep)
+        y = lax.rem(me // 2 % wide + dy, wide)
+        return (z * wide + y) * 2 + lax.rem(me % 2 + dc, 2)
+
+    near = sorted({d % deep for d in (1, 2, -1, -2)} - {0})
+    round_z = [freq_at(d, 0, 0) for d in sorted({2 % deep, -2 % deep} - {0})]
+    round_y = [freq_at(0, d, 0) for d in range(1, wide)]
+    round_core = [freq_at(0, 0, 1)]
+    greeted = [freq_at(d, 0, 0) for d in near] + round_y + round_core
     barrier = pltpu.get_barrier_semaphore()
-
-    def greet(step, carry):
-        other = lax.rem(me + step, freqs)
-        pl.semaphore_signal(barrier, inc=1, device_id={"freq": other}, device_id_type=MESH)
-        return carry
-
     for off in OFFSETS[1:]:
         other = lax.rem(lane + off, group)
         pl.semaphore_signal(barrier, inc=1, device_id={"bl": other}, device_id_type=MESH)
-    lax.fori_loop(1, freqs, greet, 0)
+    for other in greeted:
+        pl.semaphore_signal(barrier, inc=1, device_id={"freq": other}, device_id_type=MESH)
+
+    def tell(stage, others):
+        for other in others:
+            pl.semaphore_signal(rounds.at[stage], inc=1, device_id={"freq": other}, device_id_type=MESH)
+
+    def hear(stage, others):
+        if others:
+            pl.semaphore_wait(rounds.at[stage], len(others))
 
     def fill(off, coh_to, aux_to):
         chan, pol = place(lax.rem(lane + off, group))
@@ -131,11 +148,12 @@
 
     for slot in range(1, group):
         fill(OFFSETS[slot], send_coh.at[slot - 1], send_aux.at[slot - 1])
-    pl.semaphore_wait(barrier, freqs - 1 + group - 1)
+    pl.semaphore_wait(barrier, group - 1 + len(greeted))
     for slot in range(1, group):
         aux_copy(slot, OFFSETS[slot]).start()
     for slot in range(1, group):
         coh_copy(slot, OFFSETS[slot]).start()
+    tell(0, round_z)
     fill(0, coh_all.at[0], aux_all.at[0])
 
     lanes = lax.broadcasted_iota(jnp.int32, (8 * ktiles, 2 * HALF), 1)
@@ -269,6 +287,14 @@
             coh_copy(slot, 0).wait_recv()
         vector(slot)
         scatter(slot)
+        if slot == 0:
+            hear(0, round_z)
+            tell(1, round_y)
+        elif slot == 1:
+            hear(1, round_y)
+            tell(2, round_core)
+        elif slot == 2:
+            hear(2, round_core)
     update(damping[0])
     lax.fori_loop(1, damping.shape[0], one_step, 0)
 
@@ -481,6 +507,7 @@
             pltpu.VMEM((freqs, 2, 2 * per_owner, lanes), f32),
             pltpu.VMEM((2, freqs, 2, 2 * per_owner, lanes), f32),
         ] + [pltpu.SemaphoreType.DMA((n,)) for n in (group,) * 6 + (planes, 8)]
+        scratch.append(pltpu.SemaphoreType.REGULAR((3,)))
 
         def turn(value):
             return jnp.transpose(value, (0, 1, 4, 2, 3))

time: 64 us -> 61.2 us (0.956)
  Pallas kernels: 59.6 us -> 56.8 us
    pallas_call x1, Pallas kernels: 59.6 us -> 56.8 us  [step(): pl.pallas_call(functools.partial(kernel, freqs), out_shape=(out, out, out...]
where the time goes in v3:
time: 61.2 us; the launch traced here: 61.1 us
  Pallas kernels  56.8 us (93%)
  local copies, waits for them, and re-layouts  3.52 us (6%)
  between operations  0.78 us (1%)
    pallas_call x1, Pallas kernels, step(): pl.pallas_call(functools.partial(kernel, freqs), out_shape=(out, out, out...  56.8 us
    unnamed x20, local copies, waits for them, and re-layouts  3.52 us

profile of v3, /device:TPU:1, one launch (start us, length us, event | category | flops | bytes accessed | tf_op | source)
XLA Modules:
  0.0 61.1 jit_solution(2716742477408658333)
XLA Ops:
  0.6 0.0 copy-start
  0.6 0.0 copy-start.1
  0.7 0.0 copy-start.2
  0.7 0.0 copy-start.3
  0.7 0.0 copy-start.4
  0.7 0.0 copy-start.5
  0.7 0.0 copy-start.6
  0.7 0.0 copy-start.7
  0.7 1.4 %copy.12.coh = bf16[2,2,2,100,512]{4,3,2,1,0:T(8,128)(2,1)S(1)} copy(bf16[2,2,2,100,512]{4,2,3,1,0:T(2,128)(2,1)} %param.10) | data formatting | bytes 1638400 | tf_op args[1]
  2.1 0.0 copy-done
  2.1 0.0 copy-done.1
  2.1 0.0 copy-done.2
  2.1 0.0 copy-done.3
  2.2 0.0 copy-done.4
  2.2 0.0 copy-done.5
  2.2 0.0 copy-done.6
  2.2 0.0 copy-done.7
  2.2 56.8 %shard_map.112 = (f32[2,2,62,2,100]{4,3,2,1,0:T(2,128)S(1)}, f32[2,2,62,2,100]{4,3,2,1,0:T(2,128)S(1)}, f32[2,2,62,2,100]{4,3,2,1,0:T(2,128)S(1)}) custom-call(f32[2,2,2,512]{3,2,1,0:T(2,128)S(1)} %copy-done.3, bf16[2,2,2,100,512]{4,3,2,1,0:T(8,128)(2,1)S(1)} %copy.12.coh, s32[2,512]{1,0:T(2,128)S(1)} %copy-done.4, s32[2,512]{1,0:T(2,128)S(1)} %copy-done.5, ...), custom_call_target="tpu_custom_call" | custom-call | tf_op jit(solution)/shard_map/pallas_call | solution.py:517
  59.0 0.7 %copy.16 = f32[2,2,2,100,62]{3,2,4,1,0:T(2,128)} copy(f32[2,2,2,100,62]{3,2,4,1,0:T(2,128)S(1)} %bitcast.12) | data formatting | bytes 396800
  59.7 0.7 %copy.17 = f32[2,2,2,100,62]{3,2,4,1,0:T(2,128)} copy(f32[2,2,2,100,62]{3,2,4,1,0:T(2,128)S(1)} %bitcast.11) | data formatting | bytes 396800
  60.4 0.7 %copy.18 = f32[2,2,2,100,62]{3,2,4,1,0:T(2,128)} copy(f32[2,2,2,100,62]{3,2,4,1,0:T(2,128)S(1)} %bitcast.10) | data formatting | bytes 396800
Async XLA Ops:
  0.6 1.5 %copy-start = (f32[2,2,2,100,62]{3,2,4,1,0:T(2,128)S(1)}, f32[2,2,2,100,62]{3,2,4,1,0:T(2,128)}, u32[]{:S(2)}) copy-start(f32[2,2,2,100,62]{3,2,4,1,0:T(2,128)} %param.13) | copy-start | bytes 595204
  0.6 1.5 %copy-start.1 = (f32[2,2,2,100,62]{3,2,4,1,0:T(2,128)S(1)}, f32[2,2,2,100,62]{3,2,4,1,0:T(2,128)}, u32[]{:S(2)}) copy-start(f32[2,2,2,100,62]{3,2,4,1,0:T(2,128)} %param.14) | copy-start | bytes 595204
  0.7 1.5 %copy-start.2 = (f32[2,2,2,100,62]{3,2,4,1,0:T(2,128)S(1)}, f32[2,2,2,100,62]{3,2,4,1,0:T(2,128)}, u32[]{:S(2)}) copy-start(f32[2,2,2,100,62]{3,2,4,1,0:T(2,128)} %param.15) | copy-start | bytes 595204
  0.7 1.5 %copy-start.3 = (f32[2,2,2,512]{3,2,1,0:T(2,128)S(1)}, f32[2,2,2,512]{3,2,1,0:T(2,128)}, u32[]{:S(2)}) copy-start(f32[2,2,2,512]{3,2,1,0:T(2,128)} %vis.1) | copy-start | bytes 49156
  0.7 1.5 %copy-start.4 = (s32[2,512]{1,0:T(2,128)S(1)}, s32[2,512]{1,0:T(2,128)}, u32[]{:S(2)}) copy-start(s32[2,512]{1,0:T(2,128)} %pairs.1) | copy-start | bytes 12292
  0.7 1.5 %copy-start.5 = (s32[2,512]{1,0:T(2,128)S(1)}, s32[2,512]{1,0:T(2,128)}, u32[]{:S(2)}) copy-start(s32[2,512]{1,0:T(2,128)} %flags.1) | copy-start | bytes 12292
  0.7 1.5 %copy-start.6 = (f32[100]{0:T(128)S(1)}, f32[100]{0:T(128)}, u32[]{:S(2)}) copy-start(f32[100]{0:T(128)} %param.16) | copy-start | bytes 1204
  0.7 1.5 %copy-start.7 = (f32[4]{0:T(128)S(1)}, f32[4]{0:T(128)}, u32[]{:S(2)}) copy-start(f32[4]{0:T(128)} %damping.1) | copy-start | bytes 52

commit v4 on v3

--- a/solution.py
+++ b/solution.py
@@ -40,7 +40,6 @@
     damping,
     gains_out,
     cons_out,
-    dual_out,
     send_coh,
     coh_all,
     send_aux,
@@ -59,8 +58,6 @@
     gains_all,
     fwd_src,
     fwd_all,
-    part_src,
-    part_in,
     back_src,
     cons_all,
     coh_send,
@@ -69,6 +66,8 @@
     aux_recv,
     gain_send,
     gain_recv,
+    cons_send,
+    cons_recv,
     back_recv,
     misc,
     rounds,
@@ -159,6 +158,7 @@
     lanes = lax.broadcasted_iota(jnp.int32, (8 * ktiles, 2 * HALF), 1)
     low = lanes < HALF
     chan, pol = place(lane)
+    mate = lane + 1 - 2 * chan
 
     def pack(ref, to):
         to[...] = jnp.zeros_like(to)
@@ -180,8 +180,9 @@
         ids = jnp.where(ids >= HALF, ids - HALF, ids).astype(jnp.float32)
         for part in range(2):
             ones = jnp.where(ids == aux_all[slot, 2 + part : 3 + part, :], 1.0, 0.0)
-            hot[slot, :, part * rows : (part + 1) * rows] = ones.astype(jnp.bfloat16)
-            hot_t[slot, part * rows : (part + 1) * rows, :] = ones.T.astype(jnp.bfloat16)
+            at = slice((2 * slot + part) * rows, (2 * slot + part + 1) * rows)
+            hot[:, at] = ones.astype(jnp.bfloat16)
+            hot_t[at, :] = ones.T.astype(jnp.bfloat16)
 
     def spread_table():
         value = gains[...]
@@ -193,25 +194,27 @@
             both = jnp.concatenate([real[8 * k : 8 * k + 8], imag[8 * k : 8 * k + 8]], axis=0)
             table[16 * k : 16 * k + 16, :] = both.astype(jnp.bfloat16)
 
-    def gather(slot):
-        picked[slot] = jnp.dot(table[...], hot[slot], preferred_element_type=jnp.float32)
+    def gather(slot, count=1):
+        at = slice(2 * slot * rows, 2 * (slot + count) * rows)
+        picked[:, at] = jnp.dot(table[...], hot[:, at], preferred_element_type=jnp.float32)
 
     def vector(slot):
         for at in range(0, rows, WIDE):
-            first = slice(at, at + WIDE)
-            second = slice(rows + at, rows + at + WIDE)
+            sample = slice(at, at + WIDE)
+            first = slice(2 * slot * rows + at, 2 * slot * rows + at + WIDE)
+            second = slice((2 * slot + 1) * rows + at, (2 * slot + 1) * rows + at + WIDE)
 
             def load(k):
                 if 8 * k < even:
-                    cre = coh_all[slot, 8 * k : 8 * k + 8, first]
-                    cim = coh_all[slot, even + 8 * k : even + 8 * k + 8, first]
+                    cre = coh_all[slot, 8 * k : 8 * k + 8, sample]
+                    cim = coh_all[slot, even + 8 * k : even + 8 * k + 8, sample]
                 else:
-                    cre = coh_all[slot, 2 * even : 2 * even + 8, first]
+                    cre = coh_all[slot, 2 * even : 2 * even + 8, sample]
                     cim = pltpu.roll(cre, rest, 0)
-                pre = picked[slot, 16 * k : 16 * k + 8, first]
-                pim = picked[slot, 16 * k + 8 : 16 * k + 16, first]
-                qre = picked[slot, 16 * k : 16 * k + 8, second]
-                qim = picked[slot, 16 * k + 8 : 16 * k + 16, second]
+                pre = picked[16 * k : 16 * k + 8, first]
+                pim = picked[16 * k + 8 : 16 * k + 16, first]
+                qre = picked[16 * k : 16 * k + 8, second]
+                qim = picked[16 * k + 8 : 16 * k + 16, second]
                 return cre, cim, pre, pim, qre, qim
 
             mre = jnp.zeros((8, WIDE), jnp.float32)
@@ -222,8 +225,8 @@
                 tim = cim * qre - cre * qim
                 mre = mre + (pre * tre - pim * tim)
                 mim = mim + (pre * tim + pim * tre)
-            rre = aux_all[slot, 0:1, first] - jnp.sum(mre, axis=0, keepdims=True)
-            rim = aux_all[slot, 1:2, first] - jnp.sum(mim, axis=0, keepdims=True)
+            rre = aux_all[slot, 0:1, sample] - jnp.sum(mre, axis=0, keepdims=True)
+            rim = aux_all[slot, 1:2, sample] - jnp.sum(mim, axis=0, keepdims=True)
             rre = jnp.broadcast_to(rre, (8, WIDE))
             rim = jnp.broadcast_to(rim, (8, WIDE))
             held = [None, None]
@@ -239,19 +242,21 @@
                 for side, (cols, real, imag, curv) in enumerate(sides):
                     both = jnp.concatenate([real, imag], axis=0)
                     high = both.astype(jnp.bfloat16)
-                    terms[slot, 32 * k : 32 * k + 16, cols] = high
-                    terms[slot, 32 * k + 16 : 32 * k + 32, cols] = (both - high.astype(jnp.float32)).astype(jnp.bfloat16)
+                    terms[32 * k : 32 * k + 16, cols] = high
+                    terms[32 * k + 16 : 32 * k + 32, cols] = (both - high.astype(jnp.float32)).astype(jnp.bfloat16)
                     base = 32 * ktiles + 8 * (k - k % 2)
                     if k % 2:
                         both = jnp.concatenate([held[side], curv], axis=0)
-                        terms[slot, base : base + 16, cols] = both.astype(jnp.bfloat16)
+                        terms[base : base + 16, cols] = both.astype(jnp.bfloat16)
                     elif k == ktiles - 1:
                         both = jnp.concatenate([curv, jnp.zeros_like(curv)], axis=0)
-                        terms[slot, base : base + 16, cols] = both.astype(jnp.bfloat16)
+                        terms[base : base + 16, cols] = both.astype(jnp.bfloat16)
                     held[side] = curv
 
-    def scatter(slot):
-        sums[...] += jnp.dot(terms[slot], hot_t[slot], preferred_element_type=jnp.float32)
+    def scatter(slot, count=1):
+        at = slice(2 * slot * rows, 2 * (slot + count) * rows)
+        value = jnp.dot(terms[:, at], hot_t[at, :], preferred_element_type=jnp.float32)
+        sums[...] = value if slot == 0 else sums[...] + value
 
     def update(damp):
         half = lax.broadcasted_iota(jnp.int32, (8, 2 * HALF), 1) < HALF
@@ -267,17 +272,16 @@
 
     def one_step(step, carry):
         spread_table()
-        sums[...] = jnp.zeros_like(sums)
-        for slot in range(group):
-            gather(slot)
-        for slot in range(group):
-            vector(slot)
-            scatter(slot)
+        gather(0, 4)
+        vector(0)
+        vector(1)
+        vector(2)
+        vector(3)
+        scatter(0, 4)
         update(damping[step])
         return carry
 
     spread_table()
-    sums[...] = jnp.zeros_like(sums)
     for slot in range(group):
         if slot:
             aux_copy(slot, 0).wait_recv()
@@ -295,6 +299,8 @@
             tell(2, round_core)
         elif slot == 2:
             hear(2, round_core)
+            pl.semaphore_signal(rounds.at[3], inc=1, device_id={"bl": mate}, device_id_type=MESH)
+    pl.semaphore_wait(rounds.at[3], 1)
     update(damping[0])
     lax.fori_loop(1, damping.shape[0], one_step, 0)
 
@@ -306,7 +312,7 @@
     for owner in range(freqs):
         for part in range(2):
             base = part * HALF + owner * per_owner
-            fwd_src[owner, part * per_owner : (part + 1) * per_owner, :] = blend[base : base + per_owner, :]
+            fwd_src[part, owner] = blend[base : base + per_owner, :]
 
     def far_first(send):
         here = me // plane
@@ -320,17 +326,23 @@
 
             lax.fori_loop(0 if ahead else 1, plane, one, 0)
 
-    def fwd_copy(other):
+    def fwd_copy(part, other, column, way):
         return pltpu.make_async_remote_copy(
-            src_ref=fwd_src.at[other],
-            dst_ref=fwd_all.at[me],
-            send_sem=misc.at[0],
-            recv_sem=misc.at[1],
-            device_id={"freq": other},
+            src_ref=fwd_src.at[part, other],
+            dst_ref=fwd_all.at[2 * me + chan],
+            send_sem=misc.at[way],
+            recv_sem=misc.at[2],
+            device_id={"freq": other, "bl": column},
             device_id_type=MESH,
         )
 
-    far_first(lambda other: fwd_copy(other).start())
+    def send_fwd(other):
+        fwd_copy(1 - chan, other, mate, 0).start()
+        fwd_copy(chan, other, lane, 1).start()
+
+    far_first(send_fwd)
+    fwd_copy(1 - chan, me, mate, 0).start()
+    fwd_all[2 * me + chan] = fwd_src[chan, me]
 
     def gain_copy(slot, off):
         return pltpu.make_async_remote_copy(
@@ -353,55 +365,34 @@
     basis = bernstein((np.arange(total) + 0.5) / total)
     factor = np.linalg.cholesky(basis.T @ basis)
 
-    def part_copy():
-        return pltpu.make_async_remote_copy(
-            src_ref=part_src,
-            dst_ref=part_in,
-            send_sem=misc.at[2],
-            recv_sem=misc.at[3],
-            device_id={"bl": lane + 1 - 2 * lax.rem(lane, 2)},
-            device_id_type=MESH,
-        )
-
     def back_copy(other):
         return pltpu.make_async_remote_copy(
             src_ref=back_src.at[other],
-            dst_ref=cons_all.at[pol, me],
+            dst_ref=cons_all.at[lane, me],
             send_sem=misc.at[4],
             recv_sem=back_recv.at[me // plane],
             device_id={"freq": other},
             device_id_type=MESH,
         )
 
-    def swap_copy(base):
-        view = cons_all.at[pol, pl.ds(base, plane)]
+    def cons_copy(slot, off, base):
+        view = cons_all.at[lane, pl.ds(base, plane)]
         return pltpu.make_async_remote_copy(
             src_ref=view,
             dst_ref=view,
-            send_sem=misc.at[5],
-            recv_sem=misc.at[6],
-            device_id={"bl": group - 1 - lane},
+            send_sem=cons_send.at[slot],
+            recv_sem=cons_recv.at[slot],
+            device_id={"bl": lax.rem(lane + off, group)},
             device_id_type=MESH,
         )
 
-    fwd_all[me] = fwd_src[me]
-    wait_bytes(fwd_all, freqs - 1, misc.at[1])
-    for odd in range(2):
-
-        @pl.when(chan == odd)
-        def _():
-            acc = [None] * 4
-            for f in range(freqs):
-                value = fwd_all[f]
-                for m in range(4):
-                    term = value * float(basis[2 * f + odd, m])
-                    acc[m] = term if acc[m] is None else acc[m] + term
-            for m in range(4):
-                part_src[m] = acc[m]
-
-    part_copy().start()
-    part_copy().wait_recv()
-    whole = [part_src[m] + part_in[m] for m in range(4)]
+    wait_bytes(fwd_all, total - 1, misc.at[2])
+    whole = [None] * 4
+    for f in range(total):
+        value = fwd_all[f]
+        for m in range(4):
+            term = value * float(basis[f, m])
+            whole[m] = term if whole[m] is None else whole[m] + term
     forward = []
     for row in range(4):
         acc = whole[row]
@@ -421,13 +412,13 @@
                 value = value + coeffs[m] * float(basis[2 * f + odd, m])
             back_src[f, odd] = value
     far_first(lambda other: back_copy(other).start())
-    cons_all[pol, me] = back_src[me]
+    cons_all[lane, me] = back_src[me]
 
     def tiles(take):
         for part in range(2):
             for odd in range(2):
                 for n in range(stations):
-                    take(part, odd, n, n // per_owner, part * per_owner + n % per_owner)
+                    take(part, odd, n, n // per_owner, n % per_owner)
 
     for slot in range(1, group):
         gain_copy(slot, OFFSETS[slot]).wait_recv()
@@ -435,8 +426,7 @@
     def emit_gains(part, odd, n, owner, row):
         at = part * HALF + n
         tile = jnp.concatenate([gains_all[odd, at : at + 1, 0:dirs], gains_all[2 + odd, at : at + 1, 0:dirs]], axis=0)
-        gains_out[part, odd, n] = tile
-        dual_out[part, odd, n] = dual_in[part, odd, n] + tile
+        gains_out[part, odd, n] = -tile
 
     tiles(emit_gains)
 
@@ -444,17 +434,18 @@
     for ahead in sorted(range(planes), key=lambda d: min(d, planes - d)):
         from_plane = lax.rem(here + ahead, planes)
         count = plane if ahead else plane - 1
-        view = cons_all.at[pol, pl.ds(from_plane * plane, count)]
+        view = cons_all.at[lane, pl.ds(from_plane * plane, count)]
         pltpu.make_async_copy(view, view, back_recv.at[from_plane]).wait()
-        swap_copy(from_plane * plane).start()
-    wait_bytes(cons_all.at[1 - pol], freqs, misc.at[6])
+        for slot in range(1, group):
+            cons_copy(slot, OFFSETS[slot], from_plane * plane).start()
+    for slot in range(1, group):
+        wait_bytes(cons_all.at[lax.rem(lane + group - OFFSETS[slot], group)], freqs, cons_recv.at[slot])
 
     def emit_cons(part, odd, n, owner, row):
         tile = jnp.concatenate(
-            [cons_all[0, owner, odd, row : row + 1, 0:dirs], cons_all[1, owner, odd, row : row + 1, 0:dirs]], axis=0
-        )
-        cons_out[part, odd, n] = tile
-        dual_out[part, odd, n] = dual_out[part, odd, n] - tile
+            [cons_all[part, owner, odd, row : row + 1, 0:dirs], cons_all[2 + part, owner, odd, row : row + 1, 0:dirs]], axis=0
+        )
+        cons_out[part, odd, n] = -tile
 
     tiles(emit_cons)
 
@@ -462,10 +453,11 @@
         coh_copy(slot, OFFSETS[slot]).wait_send()
         aux_copy(slot, OFFSETS[slot]).wait_send()
         gain_copy(slot, OFFSETS[slot]).wait_send()
-    wait_bytes(fwd_src, freqs - 1, misc.at[0])
-    part_copy().wait_send()
+    wait_bytes(fwd_src.at[0], freqs, misc.at[0])
+    wait_bytes(fwd_src.at[0], freqs - 1, misc.at[1])
     wait_bytes(back_src, freqs - 1, misc.at[4])
-    wait_bytes(cons_all.at[pol], freqs, misc.at[5])
+    for slot in range(1, group):
+        wait_bytes(cons_all.at[lane], freqs, cons_send.at[slot])
 
 
 def solution(mesh):
@@ -488,10 +480,10 @@
             pltpu.VMEM((group, 2 * dirs, rows), f32),
             pltpu.VMEM((group - 1, 4, rows), f32),
             pltpu.VMEM((group, 4, rows), f32),
-            pltpu.VMEM((group, lanes, 2 * rows), b16),
-            pltpu.VMEM((group, 2 * rows, lanes), b16),
-            pltpu.VMEM((group, 2 * krows, 2 * rows), f32),
-            pltpu.VMEM((group, term_rows, 2 * rows), b16),
+            pltpu.VMEM((lanes, 2 * group * rows), b16),
+            pltpu.VMEM((2 * group * rows, lanes), b16),
+            pltpu.VMEM((2 * krows, 2 * group * rows), f32),
+            pltpu.VMEM((term_rows, 2 * group * rows), b16),
             pltpu.VMEM((term_rows, lanes), f32),
             pltpu.VMEM((krows, lanes), f32),
             pltpu.VMEM((krows, lanes), f32),
@@ -500,31 +492,31 @@
             pltpu.VMEM((2 * krows, lanes), b16),
             pltpu.VMEM((lanes, lanes), f32),
             pltpu.VMEM((group, lanes, lanes), f32),
-            pltpu.VMEM((freqs, 2 * per_owner, lanes), f32),
-            pltpu.VMEM((freqs, 2 * per_owner, lanes), f32),
-            pltpu.VMEM((4, 2 * per_owner, lanes), f32),
-            pltpu.VMEM((4, 2 * per_owner, lanes), f32),
-            pltpu.VMEM((freqs, 2, 2 * per_owner, lanes), f32),
-            pltpu.VMEM((2, freqs, 2, 2 * per_owner, lanes), f32),
-        ] + [pltpu.SemaphoreType.DMA((n,)) for n in (group,) * 6 + (planes, 8)]
-        scratch.append(pltpu.SemaphoreType.REGULAR((3,)))
+            pltpu.VMEM((2, freqs, per_owner, lanes), f32),
+            pltpu.VMEM((2 * freqs, per_owner, lanes), f32),
+            pltpu.VMEM((freqs, 2, per_owner, lanes), f32),
+            pltpu.VMEM((group, freqs, 2, per_owner, lanes), f32),
+        ] + [pltpu.SemaphoreType.DMA((n,)) for n in (group,) * 8 + (planes, 8)]
+        scratch.append(pltpu.SemaphoreType.REGULAR((4,)))
 
         def turn(value):
             return jnp.transpose(value, (0, 1, 4, 2, 3))
 
+        dual_whole = dual_in
         gains_in, cons_in, dual_in = turn(gains_in), turn(cons_in), turn(dual_in)
         out = jax.ShapeDtypeStruct(gains_in.shape, f32)
         outs = pl.pallas_call(
             functools.partial(kernel, freqs),
-            out_shape=(out, out, out),
+            out_shape=(out, out),
             in_specs=[whole] * 8 + [pl.BlockSpec(memory_space=pltpu.SMEM)],
-            out_specs=(whole, whole, whole),
+            out_specs=(whole, whole),
             scratch_shapes=scratch,
             compiler_params=pltpu.CompilerParams(
                 collective_id=0, has_side_effects=True, vmem_limit_bytes=40 * 1024 * 1024
             ),
         )(vis, coh, pairs, flags, gains_in, cons_in, dual_in, penalty.reshape(1, dirs), damping)
-        return tuple(jnp.transpose(value, (0, 1, 3, 4, 2)) for value in outs)
+        minus_gains, minus_cons = (jnp.transpose(value, (0, 1, 3, 4, 2)) for value in outs)
+        return (-minus_gains, -minus_cons, dual_whole - minus_gains + minus_cons)
 
     spread = P(None, "freq", None, None, None)
     return jax.shard_map(

time: 61.2 us -> 58.5 us (0.956)
  local copies, waits for them, and re-layouts: 3.52 us -> 1.43 us
  Pallas kernels: 56.8 us -> 55 us
  other arithmetic: 0 us -> 1.15 us
    unnamed x20 -> x17, local copies, waits for them, and re-layouts: 3.52 us -> 1.43 us
    pallas_call x1, Pallas kernels: 56.8 us -> 55 us  [step(): pl.pallas_call(functools.partial(kernel, freqs), out_shape=(out, out), in...]
    add x0 -> x1, other arithmetic: none -> 1.15 us  [step(): return (-minus_gains, -minus_cons, dual_whole - minus_gains + minus_cons)]
where the time goes in v4:
time: 58.5 us; the launch traced here: 58.4 us
  Pallas kernels  55 us (94%)
  local copies, waits for them, and re-layouts  1.43 us (2%)
  other arithmetic  1.15 us (2%)
  between operations  0.78 us (1%)
    pallas_call x1, Pallas kernels, step(): pl.pallas_call(functools.partial(kernel, freqs), out_shape=(out, out), in...  55 us
    unnamed x17, local copies, waits for them, and re-layouts  1.43 us

profile of v4, /device:TPU:1, one launch (start us, length us, event | category | flops | bytes accessed | tf_op | source)
XLA Modules:
  0.0 58.4 jit_solution(16819376226128684176)
XLA Ops:
  0.6 0.0 copy-start
  0.6 0.0 copy-start.1
  0.7 0.0 copy-start.2
  0.7 0.0 copy-start.3
  0.7 0.0 copy-start.4
  0.7 0.0 copy-start.5
  0.7 0.0 copy-start.6
  0.7 0.0 copy-start.7
  0.7 1.4 %copy.12.coh = bf16[2,2,2,100,512]{4,3,2,1,0:T(8,128)(2,1)S(1)} copy(bf16[2,2,2,100,512]{4,2,3,1,0:T(2,128)(2,1)} %param.10) | data formatting | bytes 1638400 | tf_op args[1]
  2.1 0.0 copy-done
  2.1 0.0 copy-done.1
  2.1 0.0 copy-done.2
  2.1 0.0 copy-done.3
  2.2 0.0 copy-done.4
  2.2 0.0 copy-done.5
  2.2 0.0 copy-done.6
  2.2 0.0 copy-done.7
  2.2 55.0 %shard_map.112 = (f32[2,2,62,2,100]{4,3,2,1,0:T(2,128)S(1)}, f32[2,2,62,2,100]{4,3,2,1,0:T(2,128)S(1)}) custom-call(f32[2,2,2,512]{3,2,1,0:T(2,128)S(1)} %copy-done.3, bf16[2,2,2,100,512]{4,3,2,1,0:T(8,128)(2,1)S(1)} %copy.12.coh, s32[2,512]{1,0:T(2,128)S(1)} %copy-done.4, s32[2,512]{1,0:T(2,128)S(1)} %copy-done.5, f32[2,2,62,2,100]{4,3,2,1,0:T(2,128)S(1)} %bitcast.13, ...), custom_call_target="tpu_custom_call" | custom-call | tf_op jit(solution)/shard_map/pallas_call | solution.py:508
  57.2 1.2 %bitcast_add_fusion = (f32[2,2,2,100,62]{3,2,4,1,0:T(2,128)}, f32[2,2,2,100,62]{3,2,4,1,0:T(2,128)}, f32[2,2,2,100,62]{3,2,4,1,0:T(2,128)}) fusion(f32[2,2,62,2,100]{4,3,2,1,0:T(2,128)S(1)} %get-tuple-element.6, f32[2,2,2,100,62]{3,2,4,1,0:T(2,128)S(1)} %copy-done, f32[2,2,62,2,100]{4,3,2,1,0:T(2,128)S(1)} %get-tuple-element.5), kind=kLoop, calls=%fused_computation | loop fusion | flops 198400 | bytes 1190400 | tf_op jit(solution)/shard_map/add | solution.py:519
Async XLA Ops:
  0.6 1.5 %copy-start = (f32[2,2,2,100,62]{3,2,4,1,0:T(2,128)S(1)}, f32[2,2,2,100,62]{3,2,4,1,0:T(2,128)}, u32[]{:S(2)}) copy-start(f32[2,2,2,100,62]{3,2,4,1,0:T(2,128)} %param.15) | copy-start | bytes 595204
  0.6 1.5 %copy-start.1 = (f32[2,2,2,100,62]{3,2,4,1,0:T(2,128)S(1)}, f32[2,2,2,100,62]{3,2,4,1,0:T(2,128)}, u32[]{:S(2)}) copy-start(f32[2,2,2,100,62]{3,2,4,1,0:T(2,128)} %param.13) | copy-start | bytes 595204
  0.7 1.5 %copy-start.2 = (f32[2,2,2,100,62]{3,2,4,1,0:T(2,128)S(1)}, f32[2,2,2,100,62]{3,2,4,1,0:T(2,128)}, u32[]{:S(2)}) copy-start(f32[2,2,2,100,62]{3,2,4,1,0:T(2,128)} %param.14) | copy-start | bytes 595204
  0.7 1.5 %copy-start.3 = (f32[2,2,2,512]{3,2,1,0:T(2,128)S(1)}, f32[2,2,2,512]{3,2,1,0:T(2,128)}, u32[]{:S(2)}) copy-start(f32[2,2,2,512]{3,2,1,0:T(2,128)} %vis.1) | copy-start | bytes 49156
  0.7 1.5 %copy-start.4 = (s32[2,512]{1,0:T(2,128)S(1)}, s32[2,512]{1,0:T(2,128)}, u32[]{:S(2)}) copy-start(s32[2,512]{1,0:T(2,128)} %pairs.1) | copy-start | bytes 12292
  0.7 1.5 %copy-start.5 = (s32[2,512]{1,0:T(2,128)S(1)}, s32[2,512]{1,0:T(2,128)}, u32[]{:S(2)}) copy-start(s32[2,512]{1,0:T(2,128)} %flags.1) | copy-start | bytes 12292
  0.7 1.5 %copy-start.6 = (f32[100]{0:T(128)S(1)}, f32[100]{0:T(128)}, u32[]{:S(2)}) copy-start(f32[100]{0:T(128)} %param.16) | copy-start | bytes 1204
  0.7 1.5 %copy-start.7 = (f32[4]{0:T(128)S(1)}, f32[4]{0:T(128)}, u32[]{:S(2)}) copy-start(f32[4]{0:T(128)} %damping.1) | copy-start | bytes 52

commit v5 on v4

--- a/solution.py
+++ b/solution.py
@@ -125,12 +125,14 @@
             aux_to[part : part + 1, :] = vis[part, chan, pl.ds(pol, 1), :] * weight
             aux_to[2 + part : 3 + part, :] = pairs[part : part + 1, :].astype(jnp.float32)
 
-    def coh_copy(slot, off):
+    def coh_copy(slot, off, at):
+        size = WIDE if slot == group - 1 else rows
+        sem = slot + at // size
         return pltpu.make_async_remote_copy(
-            src_ref=send_coh.at[slot - 1],
-            dst_ref=coh_all.at[slot],
-            send_sem=coh_send.at[slot],
-            recv_sem=coh_recv.at[slot],
+            src_ref=send_coh.at[slot - 1, :, at : at + size],
+            dst_ref=coh_all.at[slot, :, at : at + size],
+            send_sem=coh_send.at[sem],
+            recv_sem=coh_recv.at[sem],
             device_id={"bl": lax.rem(lane + off, group)},
             device_id_type=MESH,
         )
@@ -150,8 +152,9 @@
     pl.semaphore_wait(barrier, group - 1 + len(greeted))
     for slot in range(1, group):
         aux_copy(slot, OFFSETS[slot]).start()
-    for slot in range(1, group):
-        coh_copy(slot, OFFSETS[slot]).start()
+    pieces = [(slot, 0) for slot in range(1, group - 1)] + [(group - 1, at) for at in range(0, rows, WIDE)]
+    for slot, at in pieces:
+        coh_copy(slot, OFFSETS[slot], at).start()
     tell(0, round_z)
     fill(0, coh_all.at[0], aux_all.at[0])
 
@@ -198,8 +201,8 @@
         at = slice(2 * slot * rows, 2 * (slot + count) * rows)
         picked[:, at] = jnp.dot(table[...], hot[:, at], preferred_element_type=jnp.float32)
 
-    def vector(slot):
-        for at in range(0, rows, WIDE):
+    def vector(slot, start=0, stop=rows):
+        for at in range(start, stop, WIDE):
             sample = slice(at, at + WIDE)
             first = slice(2 * slot * rows + at, 2 * slot * rows + at + WIDE)
             second = slice((2 * slot + 1) * rows + at, (2 * slot + 1) * rows + at + WIDE)
@@ -229,7 +232,6 @@
             rim = aux_all[slot, 1:2, sample] - jnp.sum(mim, axis=0, keepdims=True)
             rre = jnp.broadcast_to(rre, (8, WIDE))
             rim = jnp.broadcast_to(rim, (8, WIDE))
-            held = [None, None]
             for k in range(ktiles):
                 cre, cim, pre, pim, qre, qim = load(k)
                 are = rre * cre + rim * cim
@@ -239,19 +241,14 @@
                     (first, are * qre - aim * qim, are * qim + aim * qre, square * (qre * qre + qim * qim)),
                     (second, are * pre + aim * pim, are * pim - aim * pre, square * (pre * pre + pim * pim)),
                 )
-                for side, (cols, real, imag, curv) in enumerate(sides):
+                for cols, real, imag, curv in sides:
                     both = jnp.concatenate([real, imag], axis=0)
                     high = both.astype(jnp.bfloat16)
-                    terms[32 * k : 32 * k + 16, cols] = high
-                    terms[32 * k + 16 : 32 * k + 32, cols] = (both - high.astype(jnp.float32)).astype(jnp.bfloat16)
-                    base = 32 * ktiles + 8 * (k - k % 2)
-                    if k % 2:
-                        both = jnp.concatenate([held[side], curv], axis=0)
-                        terms[base : base + 16, cols] = both.astype(jnp.bfloat16)
-                    elif k == ktiles - 1:
-                        both = jnp.concatenate([curv, jnp.zeros_like(curv)], axis=0)
-                        terms[base : base + 16, cols] = both.astype(jnp.bfloat16)
-                    held[side] = curv
+                    terms[48 * k : 48 * k + 16, cols] = high
+                    terms[48 * k + 16 : 48 * k + 32, cols] = (both - high.astype(jnp.float32)).astype(jnp.bfloat16)
+                    left = curv - curv.astype(jnp.bfloat16).astype(jnp.float32)
+                    both = jnp.concatenate([curv, left], axis=0)
+                    terms[48 * k + 32 : 48 * k + 48, cols] = both.astype(jnp.bfloat16)
 
     def scatter(slot, count=1):
         at = slice(2 * slot * rows, 2 * (slot + count) * rows)
@@ -262,10 +259,10 @@
         half = lax.broadcasted_iota(jnp.int32, (8, 2 * HALF), 1) < HALF
         for k in range(ktiles):
             at = slice(8 * k, 8 * k + 8)
-            real = sums[32 * k : 32 * k + 8, :] + sums[32 * k + 16 : 32 * k + 24, :]
-            imag = sums[32 * k + 8 : 32 * k + 16, :] + sums[32 * k + 24 : 32 * k + 32, :]
+            real = sums[48 * k : 48 * k + 8, :] + sums[48 * k + 16 : 48 * k + 24, :]
+            imag = sums[48 * k + 8 : 48 * k + 16, :] + sums[48 * k + 24 : 48 * k + 32, :]
             numer = jnp.where(half, real, imag)
-            curv = sums[32 * ktiles + 8 * k : 32 * ktiles + 8 * k + 8, :]
+            curv = sums[48 * k + 32 : 48 * k + 40, :] + sums[48 * k + 40 : 48 * k + 48, :]
             value = gains[at, :]
             pull = rate[at, :]
             gains[at, :] = value + (numer - pull * (value - target[at, :])) / (curv + damp + pull)
@@ -287,8 +284,17 @@
             aux_copy(slot, 0).wait_recv()
         hots(slot)
         gather(slot)
+        if slot == group - 1:
+            for at in range(0, rows, WIDE):
+                coh_copy(slot, 0, at).wait_recv()
+                vector(slot, at, at + WIDE)
+                for part in range(2):
+                    base = (2 * slot + part) * rows + at
+                    cols = slice(base, base + WIDE)
+                    sums[...] += jnp.dot(terms[:, cols], hot_t[cols, :], preferred_element_type=jnp.float32)
+            continue
         if slot:
-            coh_copy(slot, 0).wait_recv()
+            coh_copy(slot, 0, 0).wait_recv()
         vector(slot)
         scatter(slot)
         if slot == 0:
@@ -354,9 +360,6 @@
             device_id_type=MESH,
         )
 
-    for slot in range(1, group):
-        gain_copy(slot, OFFSETS[slot]).start()
-
     def wait_bytes(ref, count, sem):
         view = ref.at[0:count]
         pltpu.make_async_copy(view, view, sem).wait()
@@ -387,12 +390,14 @@
         )
 
     wait_bytes(fwd_all, total - 1, misc.at[2])
-    whole = [None] * 4
+    chains = [[None] * 4 for _ in range(4)]
     for f in range(total):
         value = fwd_all[f]
         for m in range(4):
             term = value * float(basis[f, m])
-            whole[m] = term if whole[m] is None else whole[m] + term
+            held = chains[m][f % 4]
+            chains[m][f % 4] = term if held is None else held + term
+    whole = [(c[0] + c[1]) + (c[2] + c[3]) for c in chains]
     forward = []
     for row in range(4):
         acc = whole[row]
@@ -412,6 +417,8 @@
                 value = value + coeffs[m] * float(basis[2 * f + odd, m])
             back_src[f, odd] = value
     far_first(lambda other: back_copy(other).start())
+    for slot in range(1, group):
+        gain_copy(slot, OFFSETS[slot]).start()
     cons_all[lane, me] = back_src[me]
 
     def tiles(take):
@@ -420,15 +427,10 @@
                 for n in range(stations):
                     take(part, odd, n, n // per_owner, n % per_owner)
 
-    for slot in range(1, group):
-        gain_copy(slot, OFFSETS[slot]).wait_recv()
-
     def emit_gains(part, odd, n, owner, row):
         at = part * HALF + n
         tile = jnp.concatenate([gains_all[odd, at : at + 1, 0:dirs], gains_all[2 + odd, at : at + 1, 0:dirs]], axis=0)
         gains_out[part, odd, n] = -tile
-
-    tiles(emit_gains)
 
     here = me // plane
     for ahead in sorted(range(planes), key=lambda d: min(d, planes - d)):
@@ -439,6 +441,9 @@
         for slot in range(1, group):
             cons_copy(slot, OFFSETS[slot], from_plane * plane).start()
     for slot in range(1, group):
+        gain_copy(slot, OFFSETS[slot]).wait_recv()
+    tiles(emit_gains)
+    for slot in range(1, group):
         wait_bytes(cons_all.at[lax.rem(lane + group - OFFSETS[slot], group)], freqs, cons_recv.at[slot])
 
     def emit_cons(part, odd, n, owner, row):
@@ -449,8 +454,9 @@
 
     tiles(emit_cons)
 
-    for slot in range(1, group):
-        coh_copy(slot, OFFSETS[slot]).wait_send()
+    for slot, at in pieces:
+        coh_copy(slot, OFFSETS[slot], at).wait_send()
+    for slot in range(1, group):
         aux_copy(slot, OFFSETS[slot]).wait_send()
         gain_copy(slot, OFFSETS[slot]).wait_send()
     wait_bytes(fwd_src.at[0], freqs, misc.at[0])
@@ -468,7 +474,7 @@
         rows = coh.shape[-1]
         ktiles = -(-dirs // 8)
         krows = 8 * ktiles
-        term_rows = 32 * ktiles + 16 * (-(-ktiles // 2))
+        term_rows = 48 * ktiles
         group = len(OFFSETS)
         per_owner = HALF // freqs
         planes = freqs // min(8, freqs)
@@ -496,7 +502,7 @@
             pltpu.VMEM((2 * freqs, per_owner, lanes), f32),
             pltpu.VMEM((freqs, 2, per_owner, lanes), f32),
             pltpu.VMEM((group, freqs, 2, per_owner, lanes), f32),
-        ] + [pltpu.SemaphoreType.DMA((n,)) for n in (group,) * 8 + (planes, 8)]
+        ] + [pltpu.SemaphoreType.DMA((n,)) for n in (group - 1 + rows // WIDE,) * 2 + (group,) * 6 + (planes, 8)]
         scratch.append(pltpu.SemaphoreType.REGULAR((4,)))
 
         def turn(value):

time: 58.5 us -> 59.1 us (1.010)
  Pallas kernels: 55 us -> 55.7 us
    pallas_call x1, Pallas kernels: 55 us -> 55.7 us  [step(): pl.pallas_call(functools.partial(kernel, freqs), out_shape=(out, out), in...]
where the time goes in v5:
time: 59.1 us; the launch traced here: 59 us
  Pallas kernels  55.7 us (94%)
  local copies, waits for them, and re-layouts  1.43 us (2%)
  other arithmetic  1.15 us (2%)
  between operations  0.78 us (1%)
    pallas_call x1, Pallas kernels, step(): pl.pallas_call(functools.partial(kernel, freqs), out_shape=(out, out), in...  55.7 us
    unnamed x17, local copies, waits for them, and re-layouts  1.43 us

profile of v5, /device:TPU:1, one launch (start us, length us, event | category | flops | bytes accessed | tf_op | source)
XLA Modules:
  0.0 59.0 jit_solution(12128038980185336864)
XLA Ops:
  0.6 0.0 copy-start
  0.6 0.0 copy-start.1
  0.7 0.0 copy-start.2
  0.7 0.0 copy-start.3
  0.7 0.0 copy-start.4
  0.7 0.0 copy-start.5
  0.7 0.0 copy-start.6
  0.7 0.0 copy-start.7
  0.7 1.4 %copy.12.coh = bf16[2,2,2,100,512]{4,3,2,1,0:T(8,128)(2,1)S(1)} copy(bf16[2,2,2,100,512]{4,2,3,1,0:T(2,128)(2,1)} %param.10) | data formatting | bytes 1638400 | tf_op args[1]
  2.1 0.0 copy-done
  2.1 0.0 copy-done.1
  2.1 0.0 copy-done.2
  2.1 0.0 copy-done.3
  2.2 0.0 copy-done.4
  2.2 0.0 copy-done.5
  2.2 0.0 copy-done.6
  2.2 0.0 copy-done.7
  2.2 55.7 %shard_map.112 = (f32[2,2,62,2,100]{4,3,2,1,0:T(2,128)S(1)}, f32[2,2,62,2,100]{4,3,2,1,0:T(2,128)S(1)}) custom-call(f32[2,2,2,512]{3,2,1,0:T(2,128)S(1)} %copy-done.3, bf16[2,2,2,100,512]{4,3,2,1,0:T(8,128)(2,1)S(1)} %copy.12.coh, s32[2,512]{1,0:T(2,128)S(1)} %copy-done.4, s32[2,512]{1,0:T(2,128)S(1)} %copy-done.5, f32[2,2,62,2,100]{4,3,2,1,0:T(2,128)S(1)} %bitcast.13, ...), custom_call_target="tpu_custom_call" | custom-call | tf_op jit(solution)/shard_map/pallas_call | solution.py:514
  57.9 1.2 %bitcast_add_fusion = (f32[2,2,2,100,62]{3,2,4,1,0:T(2,128)}, f32[2,2,2,100,62]{3,2,4,1,0:T(2,128)}, f32[2,2,2,100,62]{3,2,4,1,0:T(2,128)}) fusion(f32[2,2,62,2,100]{4,3,2,1,0:T(2,128)S(1)} %get-tuple-element.6, f32[2,2,2,100,62]{3,2,4,1,0:T(2,128)S(1)} %copy-done, f32[2,2,62,2,100]{4,3,2,1,0:T(2,128)S(1)} %get-tuple-element.5), kind=kLoop, calls=%fused_computation | loop fusion | flops 198400 | bytes 1190400 | tf_op jit(solution)/shard_map/add | solution.py:525
Async XLA Ops:
  0.6 1.5 %copy-start = (f32[2,2,2,100,62]{3,2,4,1,0:T(2,128)S(1)}, f32[2,2,2,100,62]{3,2,4,1,0:T(2,128)}, u32[]{:S(2)}) copy-start(f32[2,2,2,100,62]{3,2,4,1,0:T(2,128)} %param.15) | copy-start | bytes 595204
  0.6 1.5 %copy-start.1 = (f32[2,2,2,100,62]{3,2,4,1,0:T(2,128)S(1)}, f32[2,2,2,100,62]{3,2,4,1,0:T(2,128)}, u32[]{:S(2)}) copy-start(f32[2,2,2,100,62]{3,2,4,1,0:T(2,128)} %param.13) | copy-start | bytes 595204
  0.7 1.5 %copy-start.2 = (f32[2,2,2,100,62]{3,2,4,1,0:T(2,128)S(1)}, f32[2,2,2,100,62]{3,2,4,1,0:T(2,128)}, u32[]{:S(2)}) copy-start(f32[2,2,2,100,62]{3,2,4,1,0:T(2,128)} %param.14) | copy-start | bytes 595204
  0.7 1.5 %copy-start.3 = (f32[2,2,2,512]{3,2,1,0:T(2,128)S(1)}, f32[2,2,2,512]{3,2,1,0:T(2,128)}, u32[]{:S(2)}) copy-start(f32[2,2,2,512]{3,2,1,0:T(2,128)} %vis.1) | copy-start | bytes 49156
  0.7 1.5 %copy-start.4 = (s32[2,512]{1,0:T(2,128)S(1)}, s32[2,512]{1,0:T(2,128)}, u32[]{:S(2)}) copy-start(s32[2,512]{1,0:T(2,128)} %pairs.1) | copy-start | bytes 12292
  0.7 1.5 %copy-start.5 = (s32[2,512]{1,0:T(2,128)S(1)}, s32[2,512]{1,0:T(2,128)}, u32[]{:S(2)}) copy-start(s32[2,512]{1,0:T(2,128)} %flags.1) | copy-start | bytes 12292
  0.7 1.5 %copy-start.6 = (f32[100]{0:T(128)S(1)}, f32[100]{0:T(128)}, u32[]{:S(2)}) copy-start(f32[100]{0:T(128)} %param.16) | copy-start | bytes 1204
  0.7 1.5 %copy-start.7 = (f32[4]{0:T(128)S(1)}, f32[4]{0:T(128)}, u32[]{:S(2)}) copy-start(f32[4]{0:T(128)} %damping.1) | copy-start | bytes 52

commit v6 on v5

--- a/solution.py
+++ b/solution.py
@@ -269,12 +269,16 @@
 
     def one_step(step, carry):
         spread_table()
-        gather(0, 4)
+        gather(0)
+        gather(1, 3)
         vector(0)
+        scatter(0)
         vector(1)
+        scatter(1)
         vector(2)
+        scatter(2)
         vector(3)
-        scatter(0, 4)
+        scatter(3)
         update(damping[step])
         return carry
 

time: 59.1 us -> 59.1 us (level)
  no operation moved by 1% of the time
where the time goes in v6:
time: 59.1 us; the launch traced here: 59 us
  Pallas kernels  55.6 us (94%)
  local copies, waits for them, and re-layouts  1.43 us (2%)
  other arithmetic  1.15 us (2%)
  between operations  0.78 us (1%)
    pallas_call x1, Pallas kernels, step(): pl.pallas_call(functools.partial(kernel, freqs), out_shape=(out, out), in...  55.6 us
    unnamed x17, local copies, waits for them, and re-layouts  1.43 us

profile of v6, /device:TPU:1, one launch (start us, length us, event | category | flops | bytes accessed | tf_op | source)
XLA Modules:
  0.0 59.0 jit_solution(4412367611202144150)
XLA Ops:
  0.6 0.0 copy-start
  0.6 0.0 copy-start.1
  0.7 0.0 copy-start.2
  0.7 0.0 copy-start.3
  0.7 0.0 copy-start.4
  0.7 0.0 copy-start.5
  0.7 0.0 copy-start.6
  0.7 0.0 copy-start.7
  0.7 1.4 %copy.12.coh = bf16[2,2,2,100,512]{4,3,2,1,0:T(8,128)(2,1)S(1)} copy(bf16[2,2,2,100,512]{4,2,3,1,0:T(2,128)(2,1)} %param.10) | data formatting | bytes 1638400 | tf_op args[1]
  2.1 0.0 copy-done
  2.1 0.0 copy-done.1
  2.1 0.0 copy-done.2
  2.1 0.0 copy-done.3
  2.2 0.0 copy-done.4
  2.2 0.0 copy-done.5
  2.2 0.0 copy-done.6
  2.2 0.0 copy-done.7
  2.2 55.6 %shard_map.112 = (f32[2,2,62,2,100]{4,3,2,1,0:T(2,128)S(1)}, f32[2,2,62,2,100]{4,3,2,1,0:T(2,128)S(1)}) custom-call(f32[2,2,2,512]{3,2,1,0:T(2,128)S(1)} %copy-done.3, bf16[2,2,2,100,512]{4,3,2,1,0:T(8,128)(2,1)S(1)} %copy.12.coh, s32[2,512]{1,0:T(2,128)S(1)} %copy-done.4, s32[2,512]{1,0:T(2,128)S(1)} %copy-done.5, f32[2,2,62,2,100]{4,3,2,1,0:T(2,128)S(1)} %bitcast.13, ...), custom_call_target="tpu_custom_call" | custom-call | tf_op jit(solution)/shard_map/pallas_call | solution.py:518
  57.8 1.2 %bitcast_add_fusion = (f32[2,2,2,100,62]{3,2,4,1,0:T(2,128)}, f32[2,2,2,100,62]{3,2,4,1,0:T(2,128)}, f32[2,2,2,100,62]{3,2,4,1,0:T(2,128)}) fusion(f32[2,2,62,2,100]{4,3,2,1,0:T(2,128)S(1)} %get-tuple-element.6, f32[2,2,2,100,62]{3,2,4,1,0:T(2,128)S(1)} %copy-done, f32[2,2,62,2,100]{4,3,2,1,0:T(2,128)S(1)} %get-tuple-element.5), kind=kLoop, calls=%fused_computation | loop fusion | flops 198400 | bytes 1190400 | tf_op jit(solution)/shard_map/add | solution.py:529
Async XLA Ops:
  0.6 1.5 %copy-start = (f32[2,2,2,100,62]{3,2,4,1,0:T(2,128)S(1)}, f32[2,2,2,100,62]{3,2,4,1,0:T(2,128)}, u32[]{:S(2)}) copy-start(f32[2,2,2,100,62]{3,2,4,1,0:T(2,128)} %param.15) | copy-start | bytes 595204
  0.6 1.5 %copy-start.1 = (f32[2,2,2,100,62]{3,2,4,1,0:T(2,128)S(1)}, f32[2,2,2,100,62]{3,2,4,1,0:T(2,128)}, u32[]{:S(2)}) copy-start(f32[2,2,2,100,62]{3,2,4,1,0:T(2,128)} %param.13) | copy-start | bytes 595204
  0.7 1.5 %copy-start.2 = (f32[2,2,2,100,62]{3,2,4,1,0:T(2,128)S(1)}, f32[2,2,2,100,62]{3,2,4,1,0:T(2,128)}, u32[]{:S(2)}) copy-start(f32[2,2,2,100,62]{3,2,4,1,0:T(2,128)} %param.14) | copy-start | bytes 595204
  0.7 1.5 %copy-start.3 = (f32[2,2,2,512]{3,2,1,0:T(2,128)S(1)}, f32[2,2,2,512]{3,2,1,0:T(2,128)}, u32[]{:S(2)}) copy-start(f32[2,2,2,512]{3,2,1,0:T(2,128)} %vis.1) | copy-start | bytes 49156
  0.7 1.5 %copy-start.4 = (s32[2,512]{1,0:T(2,128)S(1)}, s32[2,512]{1,0:T(2,128)}, u32[]{:S(2)}) copy-start(s32[2,512]{1,0:T(2,128)} %pairs.1) | copy-start | bytes 12292
  0.7 1.5 %copy-start.5 = (s32[2,512]{1,0:T(2,128)S(1)}, s32[2,512]{1,0:T(2,128)}, u32[]{:S(2)}) copy-start(s32[2,512]{1,0:T(2,128)} %flags.1) | copy-start | bytes 12292
  0.7 1.5 %copy-start.6 = (f32[100]{0:T(128)S(1)}, f32[100]{0:T(128)}, u32[]{:S(2)}) copy-start(f32[100]{0:T(128)} %param.16) | copy-start | bytes 1204
  0.7 1.5 %copy-start.7 = (f32[4]{0:T(128)S(1)}, f32[4]{0:T(128)}, u32[]{:S(2)}) copy-start(f32[4]{0:T(128)} %damping.1) | copy-start | bytes 52
